TPU v7x, 128 devices: a whole 4x4x4 slice. The times are simulated.
128 devices in a mesh: queue: 16 (over x_hi, z, core), tok: 8 (over x_lo, y).
Axes of the slice: x: 4 (x_hi: 2, x_lo: 2; x = x_hi * 2 + x_lo), y: 4, z: 4, core: 2. Of those that a mesh axis runs over, the one named last changes fastest.
Arguments:
- latents: float32 [16, 1024, 64], P('queue', 'tok'), may hold values from -6 to 6
- step_index: int32 [16], replicated, may hold values from 0 to 63, as said below
- tail_noise: float32 [1024, 64], P('tok'), may hold values from -6 to 6
- patch_weight: bfloat16 [64, 1536], replicated, may hold values from -0.75 to 0.75
- time_table: float32 [64, 3, 1536], replicated, may hold values from -3 to 3
- qkv_weight: bfloat16 [1536, 4608], replicated, may hold values from -1 to 1
- q_gain: float32 [1536], replicated, may hold values from 1 to 3
- k_gain: float32 [1536], replicated, may hold values from 1 to 3
- out_weight: bfloat16 [1536, 1536], replicated, may hold values from -0.15625 to 0.15625
- head_weight: bfloat16 [1536, 64], replicated, may hold values from -0.15625 to 0.15625
Outputs:
- velocity: float32 [16, 1024, 64], P('queue', 'tok')
- queue_next: float32 [16, 1024, 64], P('queue', 'tok')
- leaving: float32 [64, 1024], P('queue', 'tok')
Inputs may be any that keep to these rules, and one draw needn't show every extreme that they name: `step_index`: strictly rising along the queue, by 1 to 4 from one frame to the next; the tail frame is at level 63.
All inputs are finite; a program needn't handle non-finite values.
Results may differ from a plain program's by a relative error of at most 0.0095.
Values may be sent and summed in bfloat16 or wider, within the bound.
A program may use at most 320 MiB of HBM per device.

v0:
```python
import jax
import jax.numpy as jnp
from jax import lax
from jax.sharding import PartitionSpec as P

HEAD_DIM = 128


def sent_together(arrays, axis, split_dim, concat_dim, along):
    columns = [a.reshape(*a.shape[:along], -1) for a in arrays]
    both = jnp.concatenate(columns, axis=along)
    filled, at, outs = (
        lax.all_to_all(both, axis, split_axis=split_dim, concat_axis=concat_dim, tiled=True),
        0,
        [],
    )
    for a, column in zip(arrays, columns):
        slab = filled[..., at : at + column.shape[along]]
        outs.append(slab.reshape(*slab.shape[:along], *a.shape[along:]))
        at += column.shape[along]
    return tuple(outs)


def passed_along(value, axis, by):
    peers = lax.axis_size(axis)
    pairs = [(i, i + by) for i in range(peers) if 0 <= i + by < peers]
    return lax.ppermute(value, axis, pairs)


def picked(value, axis, root):
    return lax.dynamic_index_in_dim(lax.all_gather(value, axis), root, 0, keepdims=False)


def layer_norm(values):
    mean_row = jnp.mean(values, axis=-1, keepdims=True)
    centred = values - mean_row
    variance = jnp.mean(centred * centred, axis=-1, keepdims=True)
    return centred * lax.rsqrt(variance + 1e-06)


def rms_norm(values, gain_vec):
    return values * lax.rsqrt(jnp.mean(values * values, axis=-1, keepdims=True) + 1e-06) * gain_vec


def fold_keys(carried, queries, portion, scaling):
    run_max, run_sum, run_out = carried
    head_count = queries.shape[1]
    head_size = queries.shape[2]
    feature = head_count * head_size
    key_rows = portion[:, :feature].reshape(portion.shape[0], head_count, head_size)
    value_rows = portion[:, feature:].reshape(portion.shape[0], head_count, head_size)
    scores = (
        jnp.einsum("rhd,khd->rhk", queries, key_rows, preferred_element_type=jnp.float32) * scaling
    )
    new_max = jnp.maximum(run_max, jnp.max(scores, axis=-1))
    weights = jnp.exp(scores - new_max[..., None])
    run_sum = jnp.sum(weights, axis=-1)
    run_out = jnp.einsum(
        "rhk,khd->rhd", weights.astype(jnp.bfloat16), value_rows, preferred_element_type=jnp.float32
    )
    return (new_max, run_sum, run_out)


def merge_states(maxima, totals, outputs):
    top = jnp.max(maxima, axis=0)
    factor = jnp.exp(maxima - top[None])
    return (top, jnp.sum(totals * factor, axis=0), jnp.sum(outputs * factor[..., None], axis=0))


def fresh_state(row_count, head_count, head_size):
    return (
        jnp.full((row_count, head_count), -1e30, jnp.float32),
        jnp.zeros((row_count, head_count), jnp.float32),
        jnp.zeros((row_count, head_count, head_size), jnp.float32),
    )


def key_value_rows(normed, qkv_weight, k_gain, feature):
    projected = jnp.dot(normed, qkv_weight[:, feature:], preferred_element_type=jnp.float32)
    key_part = rms_norm(projected[:, :feature], k_gain).astype(jnp.bfloat16)
    return jnp.concatenate([key_part, projected[:, feature:].astype(jnp.bfloat16)], axis=1)


def per_device(
    latents,
    step_index,
    tail_noise,
    patch_weight,
    time_table,
    qkv_weight,
    q_gain,
    k_gain,
    out_weight,
    head_weight,
):
    feature = patch_weight.shape[1]
    head_size = HEAD_DIM
    head_count = feature // head_size
    scaling = head_size ** (-0.5)
    levels = time_table.shape[0]
    frames = lax.axis_size("queue")
    position = lax.axis_index("queue")
    latent = latents[0]
    tok_rows = latent.shape[0]
    level_now = step_index[position]
    level_before = jnp.where(position > 0, step_index[jnp.maximum(position - 1, 0)], -1)
    one_hot = (jnp.arange(levels, dtype=jnp.int32) == level_now).astype(jnp.float32)[None, :]
    modulation = jnp.dot(
        one_hot, time_table.reshape(levels, 3 * feature), precision=lax.Precision.HIGHEST
    ).reshape(3, feature)
    hidden = jnp.dot(latent.astype(jnp.bfloat16), patch_weight, preferred_element_type=jnp.float32)
    normed = (layer_norm(hidden) * (1.0 + modulation[1]) + modulation[0]).astype(jnp.bfloat16)
    query_proj = jnp.dot(normed, qkv_weight[:, :feature], preferred_element_type=jnp.float32)
    queries = rms_norm(query_proj, q_gain).astype(jnp.bfloat16)
    key_value = key_value_rows(normed, qkv_weight, k_gain, feature)
    whole_queries = lax.all_gather(queries, "tok", axis=0, tiled=True)
    frame_rows = whole_queries.shape[0]
    whole_queries = whole_queries.reshape(frame_rows, head_count, head_size)
    state = fold_keys(
        fresh_state(frame_rows, head_count, head_size),
        whole_queries,
        lax.all_gather(key_value, "queue", axis=0, tiled=True),
        scaling,
    )
    parts = tuple(
        (
            part.astype(jnp.float32)
            for part in sent_together(
                (
                    state[0][None].astype(jnp.bfloat16),
                    state[1][None].astype(jnp.bfloat16),
                    state[2][None].astype(jnp.bfloat16),
                ),
                "tok",
                1,
                0,
                3,
            )
        )
    )
    carried = merge_states(parts[0], parts[1], parts[2])
    run_max, run_sum, run_out = carried
    attended = (run_out / run_sum[..., None]).reshape(tok_rows, feature).astype(jnp.bfloat16)
    attn_out = jnp.dot(attended, out_weight, preferred_element_type=jnp.float32)
    residual = hidden + modulation[2] * attn_out
    velocity = jnp.dot(
        residual.astype(jnp.bfloat16), head_weight, preferred_element_type=jnp.float32
    )
    sigma_now = (level_now.astype(jnp.float32) + 1.0) / levels
    sigma_next = (level_before.astype(jnp.float32) + 1.0) / levels
    updated = latent + (sigma_next - sigma_now) * velocity
    arrived = passed_along(updated.astype(jnp.bfloat16), "queue", -1).astype(updated.dtype)
    queue_next = jnp.where(position == frames - 1, tail_noise, arrived)
    clean_frame = picked(updated.T.astype(jnp.bfloat16), "queue", 0).astype(jnp.float32)
    channel_share = clean_frame.shape[0] // frames
    leaving = lax.dynamic_slice_in_dim(clean_frame, position * channel_share, channel_share, 0)
    return (velocity[None], queue_next[None], leaving)


def solution(mesh):
    placed = (P("queue", "tok", None), P(), P("tok", None), P(), P(), P(), P(), P(), P(), P())
    return jax.shard_map(
        per_device,
        mesh=mesh,
        in_specs=placed,
        out_specs=(P("queue", "tok", None), P("queue", "tok", None), P("queue", "tok")),
        check_vma=False,
    )
```

profile of v0, /device:TPU:1, one launch (start us, length us, event | category | flops | bytes accessed | tf_op | source)
XLA Modules:
  0.0 435.7 jit_solution(8018585235726513861)
XLA Ops:
  7.2 0.0 copy-start
  7.2 0.0 all-gather.6.cloned.1.call-start
  7.2 1.4 copy.69
  8.6 1.3 fusion.32
  10.0 1.2 convolution_reduce_fusion
  11.1 1.1 fusion.33
  12.3 0.2 multiply_reduce_fusion.3
  12.5 3.3 multiply_reduce_fusion.1
  15.8 0.9 multiply_convert_fusion
  16.7 0.0 all-gather.6.cloned.1.call-update
  16.8 0.0 copy-start.7
  16.8 0.0 all-gather.4.cloned.1.call-start
  16.8 5.2 %fusion.5 = f32[128,3072]{1,0:T(8,128)S(1)} fusion(bf16[1536,4608]{1,0:T(8,128)(2,1)} %param.15, f32[128,1536]{1,0:T(8,128)S(1)} %get-tuple-element.14, f32[1536]{0:T(1024)S(1)} %get-tuple-element.9, f32[1536]{0:T(1024)S(1)} %get-tuple-element.10, f32[128]{0:T(128)S(1)} %add_rsqrt_fusion.2, f32[128]{0:T(128)S(1)} %broadcast_multiply_fusion), kind=kOutput, calls=%fused_computation.6 | convolution fusion | flops 1208942592 | bytes 11809792 | tf_op jit(solution)/shard_map/dot_general | solution.py:79
  22.1 0.1 multiply_reduce_fusion.2
  22.2 0.1 multiply_convert_fusion.1
  22.4 1.0 pad_maximum_fusion.1
  23.3 0.0 all-gather.4.cloned.1.call-update
  23.4 38.3 %all-gather.6.cloned.1.call-done = bf16[1024,1536]{1,0:T(8,128)(2,1)} async-done(((bf16[128,1536]{1,0:T(8,128)(2,1)}), bf16[1024,1536]{1,0:T(8,128)(2,1)}) %all-gather.6.cloned.1.call-update) | async-done | bytes 3145744 | tf_op jit(solution)/shard_map/all_gather | solution.py:116
  61.7 3.2 copy.52
  64.9 93.0 %all-gather.4.cloned.1.call-done = bf16[2048,3072]{1,0:T(8,128)(2,1)} async-done(((bf16[128,3072]{1,0:T(8,128)(2,1)}), bf16[2048,3072]{1,0:T(8,128)(2,1)}) %all-gather.4.cloned.1.call-update) | async-done | bytes 12582928 | tf_op jit(solution)/shard_map/all_gather | solution.py:122
  157.9 10.2 %fusion.29 = (bf16[2048,1536]{1,0:T(8,128)(2,1)}, bf16[2048,1536]{1,0:T(8,128)(2,1)}) fusion(bf16[2048,3072]{1,0:T(8,128)(2,1)} %all-gather.4.cloned.1.call-done), kind=kLoop, calls=%fused_computation.56 | loop fusion | bytes 25165824 | tf_op jit(solution)/shard_map/slice | solution.py:50
  168.1 8.7 %copy.51 = bf16[2048,1536]{0,1:T(8,128)(2,1)} copy(bf16[2048,1536]{1,0:T(8,128)(2,1)} %get-tuple-element.3) | data formatting | bytes 12582912 | tf_op jit(solution)/shard_map/slice | solution.py:50
  176.8 37.0 %bitcast_reduce_fusion = (f32[1024,12]{0,1:T(8,128)S(1)}, f32[12,2048,1024]{2,1,0:T(8,128)}) fusion(bf16[2048,12,128]{0,2,1:T(8,128)(2,1)} %bitcast.80, bf16[1024,12,128]{0,2,1:T(8,128)(2,1)S(1)} %bitcast.82), kind=kOutput, calls=%fused_computation.1 | convolution fusion | flops 6492770304 | bytes 110149632 | tf_op jit(solution)/shard_map/rhd,khd->rhk/dot_general | solution.py:53
  213.8 8.7 %copy.55 = bf16[2048,1536]{0,1:T(8,128)(2,1)} copy(bf16[2048,1536]{1,0:T(8,128)(2,1)} %get-tuple-element.4) | data formatting | bytes 12582912 | tf_op jit(solution)/shard_map/slice | solution.py:51
  222.6 31.0 %fusion.2 = bf16[1024,12]{0,1:T(8,128)(2,1)S(1)} fusion(f32[12,2048,1024]{2,1,0:T(8,128)} %get-tuple-element.18, f32[1024,12]{0,1:T(8,128)S(1)} %broadcast_maximum_fusion), kind=kLoop, calls=%fused_computation.4 | loop fusion | flops 75485184 | bytes 100737024 | tf_op jit(solution)/shard_map/reduce_sum | solution.py:57
  253.6 35.0 %convert_bitcast_fusion = bf16[1,1024,12,128]{1,3,2,0:T(8,128)(2,1)S(1)} fusion(bf16[2048,12,128]{0,2,1:T(8,128)(2,1)} %bitcast.81, f32[12,2048,1024]{2,1,0:T(8,128)} %get-tuple-element.18, f32[1024,12]{0,1:T(8,128)S(1)} %broadcast_maximum_fusion), kind=kOutput, calls=%fused_computation.12 | convolution fusion | flops 6519521280 | bytes 110149632 | tf_op jit(solution)/shard_map/rhk,khd->rhd/dot_general | solution.py:58
  288.7 1.2 pad_maximum_fusion
  289.9 12.6 %copy.59 = bf16[1,1024,12,130]{3,2,0,1:T(8,128)(2,1)} copy(bf16[1,1024,12,130]{1,3,2,0:T(8,128)(2,1)S(1)} %pad_maximum_fusion) | data formatting | bytes 6389760 | tf_op jit(solution)/shard_map/concatenate | solution.py:11
  302.5 13.1 %reshape.129 = bf16[8,2,99840]{2,1,0:T(2,128)(2,1)} reshape(bf16[1024,1,12,130]{3,2,1,0:T(8,128)(2,1)} %bitcast.79) | data formatting | bytes 6389760
  315.5 4.0 all-to-all-start
  320.8 36.7 %all-to-all-done = bf16[8,2,99840]{2,1,0:T(2,128)(2,1)S(1)} async-done(((bf16[8,2,99840]{2,1,0:T(2,128)(2,1)}), bf16[8,2,99840]{2,1,0:T(2,128)(2,1)S(1)}, u32[]{:S(2)}, u32[]{:S(2)}) %all-to-all-start) | async-done | bytes 3194912 | tf_op jit(solution)/shard_map/all_to_all | solution.py:13
  357.5 10.5 %reshape.130 = bf16[1024,1,12,130]{3,2,1,0:T(8,128)(2,1)} reshape(bf16[8,2,99840]{2,1,0:T(2,128)(2,1)S(1)} %all-to-all-done) | data formatting | bytes 6389760
  368.0 7.0 %slice.61 = bf16[8,128,12,128]{3,2,1,0:T(8,128)(2,1)} slice(bf16[8,128,12,130]{3,2,1,0:T(8,128)(2,1)} %bitcast.77), slice={[0:8], [0:128], [0:12], [2:130]} | slice | bytes 6291456 | tf_op jit(solution)/shard_map/slice | solution.py:18
  374.9 4.9 %fusion.30 = (bf16[8,128,12,1]{3,2,1,0:T(8,128)(2,1)}, bf16[128,12]{1,0:T(8,128)(2,1)S(1)}, bf16[8,128,12,1]{3,2,1,0:T(8,128)(2,1)}) fusion(bf16[8,128,12,130]{3,2,1,0:T(8,128)(2,1)S(1)} %bitcast.78), kind=kLoop, calls=%fused_computation.57 | loop fusion | flops 10752 | bytes 101376 | tf_op jit(solution)/shard_map/slice | solution.py:18
  379.9 7.1 %copy.65 = bf16[8,128,12,128]{1,0,3,2:T(8,128)(2,1)S(1)} copy(bf16[8,128,12,128]{3,2,1,0:T(8,128)(2,1)} %slice.61) | data formatting | bytes 6291456
  387.0 0.0 copy-start.4
  387.0 4.6 %copy.66 = bf16[8,128,12,1]{1,0,3,2:T(8,128)(2,1)S(1)} copy(bf16[8,128,12,1]{3,2,1,0:T(8,128)(2,1)} %get-tuple-element.7) | data formatting | bytes 49152
  391.6 0.1 copy.68
  391.6 0.0 copy-start.1
  391.7 4.6 %copy.67 = bf16[8,128,12,1]{1,0,3,2:T(8,128)(2,1)S(1)} copy(bf16[8,128,12,1]{3,2,1,0:T(8,128)(2,1)} %get-tuple-element.5) | data formatting | bytes 49152
  396.3 0.0 copy-start.5
  396.4 2.0 multiply_reduce_fusion
  398.4 0.1 divide_convert_fusion
  398.5 4.3 fusion.21
  402.8 2.7 collective-permute-start
  405.4 22.2 %all-gather = bf16[1024,128]{1,0:T(8,128)(2,1)S(1)} all-gather(bf16[64,128]{1,0:T(8,128)(2,1)S(1)} %bitcast.87), channel_id=2, replica_groups=mesh['queue'=16,'tok'=8] {'queue'}, dimensions={0}, use_global_device_ids=true | all-gather | bytes 278528 | tf_op jit(solution)/shard_map/all_gather | solution.py:31
  427.6 0.6 dynamic-slice_convert_fusion
  428.2 0.6 select_bitcast_fusion
  (26 shorter events, 0.3 us)
Async XLA Ops:
  7.2 4.0 copy-start
  7.2 54.5 %all-gather.6.cloned.1.call-start = ((), (), s32[]{:S(2)}) async-start(), calls=%async_computation.2 | async-start | bytes 3538944 | tf_op jit(solution)/shard_map/all_gather | solution.py:116
  7.2 8.6 %copy-start.6 = (f32[1536]{0:T(1024)S(1)}, f32[1536]{0:T(1024)}, u32[]{:S(2)}) copy-start(f32[1536]{0:T(1024)} %param.16) | copy-start | bytes 18436
  12.3 9.7 %copy-start.3 = (f32[128,1536]{1,0:T(8,128)}, f32[128,1536]{1,0:T(8,128)S(1)}, u32[]{:S(2)}) copy-start(f32[128,1536]{1,0:T(8,128)S(1)} %get-tuple-element.14) | copy-start | bytes 2359300
  16.8 5.5 %copy-start.7 = (f32[1536]{0:T(1024)S(1)}, f32[1536]{0:T(1024)}, u32[]{:S(2)}) copy-start(f32[1536]{0:T(1024)} %param.17) | copy-start | bytes 18436
  16.8 141.1 %all-gather.4.cloned.1.call-start = ((), (), s32[]{:S(2)}) async-start(), calls=%async_computation.1 | async-start | bytes 13369344 | tf_op jit(solution)/shard_map/all_gather | solution.py:122
  315.5 42.0 %all-to-all-start = ((bf16[8,2,99840]{2,1,0:T(2,128)(2,1)}), bf16[8,2,99840]{2,1,0:T(2,128)(2,1)S(1)}, u32[]{:S(2)}, u32[]{:S(2)}) async-start(bf16[8,2,99840]{2,1,0:T(2,128)(2,1)} %reshape.129), calls=%async_computation | async-start | bytes 6389760 | tf_op jit(solution)/shard_map/all_to_all | solution.py:13
  368.0 7.0 %copy-start.2 = (bf16[1024,1,12,130]{3,2,1,0:T(8,128)(2,1)S(1)}, bf16[1024,1,12,130]{3,2,1,0:T(8,128)(2,1)}, u32[]{:S(2)}) copy-start(bf16[1024,1,12,130]{3,2,1,0:T(8,128)(2,1)} %reshape.130) | copy-start | bytes 9584644
  387.0 11.5 %copy-start.4 = (f32[1,128,64]{1,2,0:T(8,128)S(1)}, f32[1,128,64]{1,2,0:T(8,128)}, u32[]{:S(2)}) copy-start(f32[1,128,64]{1,2,0:T(8,128)} %param.10) | copy-start | bytes 98308
  391.6 37.2 %copy-start.1 = (bf16[64,1536]{1,0:T(8,128)(2,1)S(1)}, bf16[64,1536]{1,0:T(8,128)(2,1)}, u32[]{:S(2)}) copy-start(bf16[64,1536]{1,0:T(8,128)(2,1)} %param.13) | copy-start | bytes 589828
  396.3 32.0 %copy-start.5 = (f32[128,64]{0,1:T(8,128)S(1)}, f32[128,64]{0,1:T(8,128)}, u32[]{:S(2)}) copy-start(f32[128,64]{0,1:T(8,128)} %param.12) | copy-start | bytes 98308
  402.8 25.5 %collective-permute-start = (bf16[128,64]{0,1:T(8,128)(2,1)S(1)}, bf16[128,64]{0,1:T(8,128)(2,1)S(1)}, u32[]{:S(2)}, u32[]{:S(2)}) collective-permute-start(bf16[128,64]{0,1:T(8,128)(2,1)S(1)} %get-tuple-element.19), channel_id=1, source_target_pairs={{8,0},{16,8},{24,16},{32,24},{40,32},{48,40},{56,48},{64,56},{72,6... | collective-permute-start | bytes 49160 | tf_op jit(solution)/shard_map/ppermute | solution.py:27
Sparse Core Ops, SparseCore 0:
  16.9 44.7 all-gather.5
  64.2 93.6 all-gather.3
where the time goes:
time: 437 us; the launch traced here: 436 us
  waiting for transfers between devices  168 us (38%)
  local copies, waits for them, and re-layouts  93.1 us (21%)
  matrix products  87 us (20%)
  other arithmetic  43 us (10%)
  blocking collectives  22.2 us (5%)
  between operations  15.6 us (4%)
  starting transfers between devices  6.78 us (2%)
    all_gather x1, waiting for transfers between devices, per_device(): lax.all_gather(key_value, 'queue', axis=0, tiled=True)  93 us
    unnamed x22, local copies, waits for them, and re-layouts  39.9 us
    all_gather x1, waiting for transfers between devices, per_device(): whole_queries = lax.all_gather(queries, 'tok', axis=0, tiled=True)  38.3 us
    dot_general x1, matrix products, fold_keys(): jnp.einsum('rhd,khd->rhk', queries, key_rows, preferred_element_type=jnp....  37 us
    all_to_all x1, waiting for transfers between devices, sent_together(): lax.all_to_all(both, axis, split_axis=split_dim, concat_axis=concat_dim,...  36.7 us
    dot_general x1, matrix products, fold_keys(): jnp.einsum('rhk,khd->rhd', weights.astype(jnp.bfloat16), value_rows, pref...  35 us
    reduce_sum x1, other arithmetic, fold_keys(): run_sum = jnp.sum(weights, axis=-1)  31 us
    all_gather x1, blocking collectives, picked(): lax.all_gather(value, axis)  22.2 us
  transfers between devices with their start and end apart: 4, of which 3 were waited for; matrix products, arithmetic and copies ran while one was open for 2% of the time, Pallas kernels for 0%

commit v1 on v0

--- a/solution.py
+++ b/solution.py
@@ -1,9 +1,15 @@
 import jax
 import jax.numpy as jnp
 from jax import lax
+from jax.experimental import pallas as pl
+from jax.experimental.pallas import tpu as pltpu
 from jax.sharding import PartitionSpec as P
 
 HEAD_DIM = 128
+LOG2E = 1.4426950408889634
+SAFE_LOG2 = 112.0
+VALUE_SHRINK = 0.0625
+MESH_ID = pl.DeviceIdType.MESH
 
 
 def sent_together(arrays, axis, split_dim, concat_dim, along):
@@ -81,7 +87,7 @@
     return jnp.concatenate([key_part, projected[:, feature:].astype(jnp.bfloat16)], axis=1)
 
 
-def per_device(
+def careful(
     latents,
     step_index,
     tail_noise,
@@ -157,6 +163,309 @@
     return (velocity[None], queue_next[None], leaving)
 
 
+def dot_nt(a, b):
+    return lax.dot_general(a, b, (((1,), (1,)), ((), ())), preferred_element_type=jnp.float32)
+
+
+def attention_kernel(q_in, kv_in, out, q_all, kv_all, o_send, o_recv, a_send,
+                     xq_s, xq_r, xk_s, xk_r, yq_s, yq_r, zk_s, zk_r, ck_s, ck_r,
+                     oy_s, oy_r, ox_s, ox_r):
+    queue = lax.axis_index("queue")
+    tok = lax.axis_index("tok")
+    core = lax.rem(queue, 2)
+    z = lax.rem(queue // 2, 4)
+    x = (queue // 8) * 2 + tok // 4
+    y = lax.rem(tok, 4)
+
+    def device(px, py, pz, pc):
+        return (((px // 2) * 4 + pz) * 2 + pc, lax.rem(px, 2) * 4 + py)
+
+    def hop(v, d):
+        return lax.rem(v + d + 4, 4)
+
+    slot = z * 2 + core
+
+    def rows(n, size):
+        return pl.ds(pl.multiple_of(n * size, size), size)
+
+    def remote(src, dst, s, r, dev):
+        return pltpu.make_async_remote_copy(src_ref=src, dst_ref=dst, send_sem=s, recv_sem=r,
+                                            device_id=dev, device_id_type=MESH_ID)
+
+    def x_query(h, d):
+        g = hop(x, d)
+        return remote(q_in.at[g * 3 + h], q_all.at[h, y, rows(x, 128)],
+                      xq_s.at[h, d], xq_r.at[h, d], device(g, y, z, core))
+
+    def x_query_in(h, d):
+        g = hop(x, -d)
+        return remote(q_in.at[x * 3 + h], q_all.at[h, y, rows(g, 128)],
+                      xq_s.at[h, d], xq_r.at[h, d], device(g, y, z, core))
+
+    def x_keys(h, d):
+        g = hop(x, d)
+        return remote(kv_in.at[g * 3 + h], kv_all.at[h, :, rows(slot * 4 + x, 128)],
+                      xk_s.at[h, d], xk_r.at[h, d], device(g, y, z, core))
+
+    def x_keys_in(h, d):
+        g = hop(x, -d)
+        return remote(kv_in.at[x * 3 + h], kv_all.at[h, :, rows(slot * 4 + g, 128)],
+                      xk_s.at[h, d], xk_r.at[h, d], device(g, y, z, core))
+
+    def y_query(h, d):
+        return remote(q_all.at[h, y], q_all.at[h, y], yq_s.at[h, d], yq_r.at[h, d],
+                      device(x, hop(y, d), z, core))
+
+    def y_query_in(h, d):
+        g = hop(y, -d)
+        return remote(q_all.at[h, g], q_all.at[h, g], yq_s.at[h, d], yq_r.at[h, d],
+                      device(x, g, z, core))
+
+    def z_keys(h, d):
+        at = kv_all.at[h, :, rows(slot, 512)]
+        return remote(at, at, zk_s.at[h, d], zk_r.at[h, d], device(x, y, hop(z, d), core))
+
+    def z_keys_in(h, d):
+        g = hop(z, -d)
+        at = kv_all.at[h, :, rows(g * 2 + core, 512)]
+        return remote(at, at, zk_s.at[h, d], zk_r.at[h, d], device(x, y, g, core))
+
+    def c_keys(h, d):
+        at = kv_all.at[h, :, rows(hop(z, -d) * 2 + core, 512)]
+        return remote(at, at, ck_s.at[h, d], ck_r.at[h, d], device(x, y, z, 1 - core))
+
+    def c_keys_in(h, d):
+        at = kv_all.at[h, :, rows(hop(z, -d) * 2 + 1 - core, 512)]
+        return remote(at, at, ck_s.at[h, d], ck_r.at[h, d], device(x, y, z, 1 - core))
+
+    def y_part(h, d):
+        return remote(o_send.at[h, hop(y, d)], o_recv.at[h, y], oy_s.at[h, d], oy_r.at[h, d],
+                      device(x, hop(y, d), z, core))
+
+    def y_part_in(h, d):
+        g = hop(y, -d)
+        return remote(o_send.at[h, g], o_recv.at[h, g], oy_s.at[h, d], oy_r.at[h, d],
+                      device(x, g, z, core))
+
+    def x_back(h, d):
+        g = hop(x, d)
+        return remote(a_send.at[h, g], out.at[x * 3 + h], ox_s.at[h, d], ox_r.at[h, d],
+                      device(g, y, z, core))
+
+    def x_back_in(h, d):
+        g = hop(x, -d)
+        return remote(a_send.at[h, g], out.at[g * 3 + h], ox_s.at[h, d], ox_r.at[h, d],
+                      device(g, y, z, core))
+
+    barrier = pltpu.get_barrier_semaphore()
+    for d in (1, 2, 3):
+        for dev in (device(hop(x, d), y, z, core), device(x, hop(y, d), z, core),
+                    device(x, y, hop(z, d), core)):
+            pl.semaphore_signal(barrier, inc=1, device_id=dev, device_id_type=MESH_ID)
+    pl.semaphore_signal(barrier, inc=1, device_id=device(x, y, z, 1 - core),
+                        device_id_type=MESH_ID)
+    pl.semaphore_wait(barrier, 10)
+
+    for h in range(3):
+        for d in (1, 3, 2):
+            x_keys(h, d).start()
+        for d in (1, 3, 2):
+            x_query(h, d).start()
+    for h in range(3):
+        q_all[h, y, rows(x, 128), :] = q_in[x * 3 + h]
+        for kv in range(2):
+            kv_all[h, kv, rows(slot * 4 + x, 128), :] = kv_in[x * 3 + h, kv]
+
+    def spread(h):
+        for d in (1, 3, 2):
+            x_keys_in(h, d).wait_recv()
+        for d in (1, 3, 2):
+            z_keys(h, d).start()
+        c_keys(h, 0).start()
+        for d in (1, 3, 2):
+            x_query_in(h, d).wait_recv()
+        for d in (1, 3, 2):
+            y_query(h, d).start()
+
+    def share(h, d):
+        z_keys_in(h, d).wait_recv()
+        c_keys(h, d).start()
+
+    for h in range(3):
+        spread(h)
+    for d in (1, 3, 2):
+        share(0, d)
+    for d in (0, 1, 3, 2):
+        c_keys_in(0, d).wait_recv()
+
+    def combine(h):
+        for d in (1, 2, 3):
+            y_part_in(h, d).wait_recv()
+        parts = [o_send.at[h, y]] + [o_recv.at[h, hop(y, d)] for d in (1, 2, 3)]
+        den = jnp.zeros((4, 128), jnp.float32)
+        for part in parts:
+            tail = part[512:528, :].astype(jnp.float32)
+            den = den + (tail[0:4] + tail[4:8])
+        inv = (1.0 / VALUE_SHRINK) / den
+        for g in range(4):
+            num = parts[0][g * 128:(g + 1) * 128, :].astype(jnp.float32)
+            for part in parts[1:]:
+                num = num + part[g * 128:(g + 1) * 128, :].astype(jnp.float32)
+            column = jnp.transpose(jnp.broadcast_to(inv[g:g + 1, :], (128, 128)))
+            a_send[h, g] = (num * column).astype(jnp.bfloat16)
+        out[x * 3 + h] = a_send[h, x]
+        for d in (1, 3, 2):
+            x_back(h, d).start()
+
+    def chunk(t, carry):
+        h, i = t // 4, lax.rem(t, 4)
+        to = lax.rem(y + i + 1, 4)
+
+        @pl.when(i < 3)
+        def _():
+            y_query_in(h, 3 - i).wait_recv()
+
+        queries = q_all[h, to]
+        scores = dot_nt(queries, kv_all[h, 0])
+        weights = jnp.exp2(scores)
+        total = weights[:, 0:128]
+        for n in range(1, 32):
+            total = total + weights[:, n * 128:(n + 1) * 128]
+        num = jnp.dot(weights.astype(jnp.bfloat16), kv_all[h, 1],
+                      preferred_element_type=jnp.float32)
+        o_send[h, to, 0:512, :] = num.astype(jnp.bfloat16)
+        rows_of = [jnp.sum(jnp.transpose(total[g * 128:(g + 1) * 128, :]), axis=0, keepdims=True)
+                   for g in range(4)]
+        den = jnp.concatenate(rows_of, axis=0)
+        high = den.astype(jnp.bfloat16).astype(jnp.float32)
+        tail = jnp.concatenate([high, den - high, jnp.zeros((8, 128), jnp.float32)], axis=0)
+        o_send[h, to, 512:528, :] = tail.astype(jnp.bfloat16)
+
+        @pl.when(i < 3)
+        def _():
+            y_part(h, i + 1).start()
+
+        @pl.when(jnp.logical_and(h < 2, i == 1))
+        def _():
+            share(h + 1, 1)
+            share(h + 1, 3)
+
+        @pl.when(jnp.logical_and(h < 2, i == 2))
+        def _():
+            share(h + 1, 2)
+
+        @pl.when(jnp.logical_and(h < 2, i == 3))
+        def _():
+            for d in (0, 1, 3, 2):
+                c_keys_in(h + 1, d).wait_recv()
+
+        @pl.when(jnp.logical_and(h > 0, i == 1))
+        def _():
+            combine(h - 1)
+
+        return carry
+
+    lax.fori_loop(0, 12, chunk, 0)
+    combine(2)
+    for h in range(3):
+        for d in (1, 3, 2):
+            x_back_in(h, d).wait_recv()
+    for h in range(3):
+        for d in (1, 2, 3):
+            x_keys(h, d).wait_send()
+            x_query(h, d).wait_send()
+            y_query(h, d).wait_send()
+            z_keys(h, d).wait_send()
+            y_part(h, d).wait_send()
+            x_back(h, d).wait_send()
+        for d in range(4):
+            c_keys(h, d).wait_send()
+
+
+def attention(q_in, kv_in):
+    sems = [pltpu.SemaphoreType.DMA((3, 4))] * 14
+    return pl.pallas_call(
+        attention_kernel,
+        out_shape=jax.ShapeDtypeStruct((12, 128, 128), jnp.bfloat16),
+        in_specs=[pl.BlockSpec(memory_space=pltpu.VMEM)] * 2,
+        out_specs=pl.BlockSpec(memory_space=pltpu.VMEM),
+        scratch_shapes=[
+            pltpu.VMEM((3, 4, 512, 128), jnp.bfloat16),
+            pltpu.VMEM((3, 2, 4096, 128), jnp.bfloat16),
+            pltpu.VMEM((3, 4, 528, 128), jnp.bfloat16),
+            pltpu.VMEM((3, 4, 528, 128), jnp.bfloat16),
+            pltpu.VMEM((3, 4, 128, 128), jnp.bfloat16),
+        ] + sems,
+        compiler_params=pltpu.CompilerParams(
+            collective_id=1, has_side_effects=True, vmem_limit_bytes=56 * 2**20),
+        cost_estimate=pl.CostEstimate(flops=13 * 10**9, bytes_accessed=20 * 10**6,
+                                      transcendentals=25 * 10**6),
+    )(q_in, kv_in)
+
+
+def per_device(
+    latents,
+    step_index,
+    tail_noise,
+    patch_weight,
+    time_table,
+    qkv_weight,
+    q_gain,
+    k_gain,
+    out_weight,
+    head_weight,
+):
+    feature = patch_weight.shape[1]
+    heads = feature // HEAD_DIM
+    levels = time_table.shape[0]
+    frames = lax.axis_size("queue")
+    position = lax.axis_index("queue")
+    latent = latents[0]
+    level_now = step_index[position]
+    level_before = jnp.where(position > 0, step_index[jnp.maximum(position - 1, 0)], -1)
+    modulation = lax.dynamic_index_in_dim(time_table, level_now, 0, keepdims=False)
+    hidden = jnp.dot(latent.astype(jnp.bfloat16), patch_weight, preferred_element_type=jnp.float32)
+    normed = (layer_norm(hidden) * (1.0 + modulation[1]) + modulation[0]).astype(jnp.bfloat16)
+    projected = jnp.dot(normed, qkv_weight, preferred_element_type=jnp.float32)
+    scale = HEAD_DIM ** (-0.5) * LOG2E
+    queries = (rms_norm(projected[:, :feature], q_gain) * scale).astype(jnp.bfloat16)
+    keys = rms_norm(projected[:, feature:2 * feature], k_gain).astype(jnp.bfloat16)
+    values = (projected[:, 2 * feature:] * VALUE_SHRINK).astype(jnp.bfloat16)
+
+    def by_head(a):
+        return a.reshape(-1, heads, HEAD_DIM).transpose(1, 0, 2)
+
+    q_heads, k_heads, v_heads = by_head(queries), by_head(keys), by_head(values)
+
+    def top_norm(a):
+        wide = a.astype(jnp.float32)
+        return jnp.max(jnp.sum(wide * wide, axis=-1), axis=-1)
+
+    sizes = jnp.stack([top_norm(q_heads), top_norm(k_heads),
+                       jnp.max(jnp.abs(v_heads.astype(jnp.float32)), axis=(1, 2))])
+    sizes = lax.pmax(sizes, ("queue", "tok"))
+    plain = jnp.logical_and(jnp.all(jnp.sqrt(sizes[0]) * jnp.sqrt(sizes[1]) <= SAFE_LOG2),
+                            jnp.all(sizes[2] <= 2.0))
+    attended = attention(q_heads, jnp.stack([k_heads, v_heads], axis=1))
+    attended = attended.transpose(1, 0, 2).reshape(-1, feature)
+    attn_out = jnp.dot(attended, out_weight, preferred_element_type=jnp.float32)
+    residual = hidden + modulation[2] * attn_out
+    velocity = jnp.dot(
+        residual.astype(jnp.bfloat16), head_weight, preferred_element_type=jnp.float32
+    )
+    sigma_now = (level_now.astype(jnp.float32) + 1.0) / levels
+    sigma_next = (level_before.astype(jnp.float32) + 1.0) / levels
+    updated = latent + (sigma_next - sigma_now) * velocity
+    arrived = passed_along(updated.astype(jnp.bfloat16), "queue", -1).astype(updated.dtype)
+    queue_next = jnp.where(position == frames - 1, tail_noise, arrived)
+    clean_frame = picked(updated.T.astype(jnp.bfloat16), "queue", 0).astype(jnp.float32)
+    channel_share = clean_frame.shape[0] // frames
+    leaving = lax.dynamic_slice_in_dim(clean_frame, position * channel_share, channel_share, 0)
+    args = (latents, step_index, tail_noise, patch_weight, time_table, qkv_weight, q_gain,
+            k_gain, out_weight, head_weight)
+    return lax.cond(plain, lambda *_: (velocity[None], queue_next[None], leaving), careful, *args)
+
+
 def solution(mesh):
     placed = (P("queue", "tok", None), P(), P("tok", None), P(), P(), P(), P(), P(), P(), P())
     return jax.shard_map(

time: 437 us -> 636 us (1.46); the launches traced: 436 us -> 627 us
  blocking collectives: 22.2 us -> 111 us
  Pallas kernels: 0 us -> 70 us
  starting transfers between devices: 6.78 us -> 22.5 us
  matrix products: 87 us -> 98.7 us
  waiting for transfers between devices: 168 us -> 161 us
    pallas_call x0 -> x1, Pallas kernels: none -> 70 us  [attention(): pl.pallas_call(attention_kernel, out_shape=jax.ShapeDtypeStruct((12, 128,...]
    pmax x0 -> x1, blocking collectives: none -> 64 us  [per_device(): sizes = lax.pmax(sizes, ('queue', 'tok'))]
    cond x0 -> x18, local copies, waits for them, and re-layouts: none -> 39.9 us
    unnamed x22 -> x16, local copies, waits for them, and re-layouts: 39.9 us -> 0.04 us
    all_gather x1 -> x2, blocking collectives: 22.2 us -> 46.7 us  [picked(): lax.all_gather(value, axis)]
    dot_general x2 -> x5, matrix products: 4.43 us -> 16.2 us  [the longest x1 7.14 us: per_device(): projected = jnp.dot(normed, qkv_weight, preferred_element_type=jnp.float32)]
    all_gather x2, starting transfers between devices: 0.08 us -> 11.4 us  [the longest x1 11.3 us: careful(): whole_queries = lax.all_gather(queries, 'tok', axis=0, tiled=True)]
    all_gather x2, waiting for transfers between devices: 131 us -> 124 us  [the longest x1 93 us: careful(): lax.all_gather(key_value, 'queue', axis=0, tiled=True)]
  transfers between devices with their start and end apart: 4 -> 5, of which waited for: 3 -> 3; matrix products, arithmetic and copies ran while one was open for 2% -> 2% of each run, Pallas kernels for 0% -> 0%
where the time goes in v1:
time: 636 us; the launch traced here: 627 us
  waiting for transfers between devices  161 us (25%)
  blocking collectives  111 us (17%)
  matrix products  98.7 us (16%)
  local copies, waits for them, and re-layouts  95.1 us (15%)
  Pallas kernels  70 us (11%)
  other arithmetic  48.3 us (8%)
  starting transfers between devices  22.5 us (4%)
  between operations  19.3 us (3%)
    all_gather x1, waiting for transfers between devices, careful(): lax.all_gather(key_value, 'queue', axis=0, tiled=True)  93 us
    pallas_call x1, Pallas kernels, attention(): pl.pallas_call(attention_kernel, out_shape=jax.ShapeDtypeStruct((12, 128,...  70 us
    pmax x1, blocking collectives, per_device(): sizes = lax.pmax(sizes, ('queue', 'tok'))  64 us
    all_gather x2, blocking collectives, picked(): lax.all_gather(value, axis)  46.7 us
    cond x18, local copies, waits for them, and re-layouts  39.9 us
    dot_general x1, matrix products, fold_keys(): jnp.einsum('rhd,khd->rhk', queries, key_rows, preferred_element_type=jnp....  37 us
    all_to_all x1, waiting for transfers between devices, sent_together(): lax.all_to_all(both, axis, split_axis=split_dim, concat_axis=concat_dim,...  36.7 us
    dot_general x1, matrix products, fold_keys(): jnp.einsum('rhk,khd->rhd', weights.astype(jnp.bfloat16), value_rows, pref...  35 us
  transfers between devices with their start and end apart: 5, of which 3 were waited for; matrix products, arithmetic and copies ran while one was open for 2% of the time, Pallas kernels for 0%

profile of v1, /device:TPU:1, one launch (start us, length us, event | category | flops | bytes accessed | tf_op | source)
XLA Modules:
  0.0 627.0 jit_solution(7079792962589480028)
XLA Ops:
  7.2 1.3 fusion.48
  10.4 1.3 fusion.49
  12.7 0.9 dynamic-slice_reduce_fusion
  13.6 7.1 %fusion.32 = f32[128,4608]{1,0:T(8,128)S(1)} fusion(bf16[1536,4608]{1,0:T(8,128)(2,1)} %param.17, f32[128,1536]{1,0:T(8,128)S(1)} %get-tuple-element.161, f32[1536]{0:T(1024)S(1)} %get-tuple-element.133, f32[1536]{0:T(1024)S(1)} %get-tuple-element.134, f32[128]{0:T(128)S(1)} %add_rsqrt_fusion.5, f32[128]{0:T(128)S(1)} %broadcast_multiply_fusion.1), kind=kOutput, calls=%fused_computation.74 | convolution fusion | flops 1812922368 | bytes 17314816 | tf_op jit(solution)/shard_map/dot_general | solution.py:429
  24.3 0.9 pad_maximum_fusion.2.kv_in
  25.3 70.0 %shard_map.127 = bf16[12,128,128]{2,1,0:T(8,128)(2,1)} custom-call(bf16[12,128,128]{2,1,0:T(8,128)(2,1)} %bitcast.133, bf16[12,2,128,128]{3,2,1,0:T(8,128)(2,1)} %pad_maximum_fusion.2.kv_in), custom_call_target="tpu_custom_call" | custom-call | flops 12999999488 | bytes 20000000 | tf_op jit(solution)/shard_map/pallas_call | solution.py:387
  95.3 1.3 copy.117
  96.7 4.1 fusion.38
  100.7 4.5 collective-permute-start.1
  105.2 64.0 %pmax.7 = f32[3,12]{1,0:T(4,128)S(1)} all-reduce(f32[3,12]{1,0:T(4,128)S(1)} %pad_maximum_fusion.3), channel_id=1, replica_groups=mesh['queue'=16,'tok'=8] {'queue','tok'}, use_global_device_ids=true, to_apply=%region_9.10 | all-reduce | flops 36 | bytes 288 | tf_op jit(solution)/shard_map/pmax | solution.py:446
  169.2 24.5 %all-gather.1 = bf16[1024,128]{1,0:T(8,128)(2,1)} all-gather(bf16[64,128]{1,0:T(8,128)(2,1)S(1)} %bitcast.143), channel_id=3, replica_groups=mesh['queue'=16,'tok'=8] {'queue'}, dimensions={0}, use_global_device_ids=true | all-gather | bytes 278528 | tf_op jit(solution)/shard_map/all_gather | solution.py:37
  193.7 0.6 compare_reduce_fusion
  195.7 0.6 convert_element_type.167
  196.3 423.5 %conditional.1 = (f32[1,128,64]{1,2,0:T(8,128)}, f32[1,128,64]{1,2,0:T(8,128)}, f32[4,128]{1,0:T(4,128)}) conditional(s32[]{:T(128)} %convert_element_type.162, (f32[1,128,64]{1,2,0:T(8,128)S(1)}, bf16[64,1536]{1,0:T(8,128)(2,1)S(1)}, s32[16]{0:T(128)S(1)}, f32[64,3,1536]{2,0,1:T(8,128)S(1)}, bf16[1536,4608]{1,0:T(8,128)(2,1)}, ...), branch_computations={%region_12.22_spmd, %region_22.23_spmd} | conditional | flops 15579123712 | bytes 533929024 | solution.py:466
  196.3 11.3 %all-gather.7.cloned.1.call-start = ((), (), s32[]{:S(2)}) async-start(), calls=%async_computation.2 | async-start | bytes 3538944 | tf_op jit(solution)/shard_map/cond/branch_0_fun/all_gather | solution.py:122
  207.7 0.6 fusion.46
  208.4 1.1 convolution_reduce_fusion
  209.5 0.6 fusion.45
  210.7 3.3 multiply_reduce_fusion.1
  214.0 0.9 multiply_convert_fusion
  215.0 5.2 fusion.5
  220.6 1.0 pad_maximum_fusion.1
  221.6 30.8 %all-gather.7.cloned.1.call-done = bf16[1024,1536]{1,0:T(8,128)(2,1)} async-done(((bf16[128,1536]{1,0:T(8,128)(2,1)}), bf16[1024,1536]{1,0:T(8,128)(2,1)}) %all-gather.7.cloned.1.call-update) | async-done | bytes 3145744 | tf_op jit(solution)/shard_map/cond/branch_0_fun/all_gather | solution.py:122
  252.4 3.2 copy.102
  255.5 93.0 %all-gather.5.cloned.1.call-done = bf16[2048,3072]{1,0:T(8,128)(2,1)} async-done(((bf16[128,3072]{1,0:T(8,128)(2,1)}), bf16[2048,3072]{1,0:T(8,128)(2,1)}) %all-gather.5.cloned.1.call-update) | async-done | bytes 12582928 | tf_op jit(solution)/shard_map/cond/branch_0_fun/all_gather | solution.py:128
  348.6 10.2 %fusion.43 = (bf16[2048,1536]{1,0:T(8,128)(2,1)}, bf16[2048,1536]{1,0:T(8,128)(2,1)}) fusion(bf16[2048,3072]{1,0:T(8,128)(2,1)} %all-gather.5.cloned.1.call-done), kind=kLoop, calls=%fused_computation.95 | loop fusion | bytes 25165824 | tf_op jit(solution)/shard_map/cond/branch_0_fun/slice | solution.py:56
  358.8 8.7 %copy.101 = bf16[2048,1536]{0,1:T(8,128)(2,1)} copy(bf16[2048,1536]{1,0:T(8,128)(2,1)} %get-tuple-element.137) | data formatting | bytes 12582912 | tf_op jit(solution)/shard_map/cond/branch_0_fun/slice | solution.py:56
  367.5 37.0 %bitcast_reduce_fusion = (f32[1024,12]{0,1:T(8,128)S(1)}, f32[12,2048,1024]{2,1,0:T(8,128)}) fusion(bf16[2048,12,128]{0,2,1:T(8,128)(2,1)} %bitcast.127, bf16[1024,12,128]{0,2,1:T(8,128)(2,1)S(1)} %bitcast.129), kind=kOutput, calls=%fused_computation.3 | convolution fusion | flops 6492770304 | bytes 110149632 | tf_op jit(solution)/shard_map/cond/branch_0_fun/rhd,khd->rhk/dot_general | solution.py:59
  404.5 8.7 %copy.105 = bf16[2048,1536]{0,1:T(8,128)(2,1)} copy(bf16[2048,1536]{1,0:T(8,128)(2,1)} %get-tuple-element.138) | data formatting | bytes 12582912 | tf_op jit(solution)/shard_map/cond/branch_0_fun/slice | solution.py:57
  413.2 31.0 %fusion.2 = bf16[1024,12]{0,1:T(8,128)(2,1)S(1)} fusion(f32[12,2048,1024]{2,1,0:T(8,128)} %get-tuple-element.152, f32[1024,12]{0,1:T(8,128)S(1)} %broadcast_maximum_fusion), kind=kLoop, calls=%fused_computation.6 | loop fusion | flops 75485184 | bytes 100737024 | tf_op jit(solution)/shard_map/cond/branch_0_fun/reduce_sum | solution.py:63
  444.3 35.0 %convert_bitcast_fusion.1 = bf16[1,1024,12,128]{1,3,2,0:T(8,128)(2,1)S(1)} fusion(bf16[2048,12,128]{0,2,1:T(8,128)(2,1)} %bitcast.128, f32[12,2048,1024]{2,1,0:T(8,128)} %get-tuple-element.152, f32[1024,12]{0,1:T(8,128)S(1)} %broadcast_maximum_fusion), kind=kOutput, calls=%fused_computation.14 | convolution fusion | flops 6519521280 | bytes 110149632 | tf_op jit(solution)/shard_map/cond/branch_0_fun/rhk,khd->rhd/dot_general | solution.py:64
  479.4 1.2 pad_maximum_fusion
  480.6 12.6 %copy.109 = bf16[1,1024,12,130]{3,2,0,1:T(8,128)(2,1)} copy(bf16[1,1024,12,130]{1,3,2,0:T(8,128)(2,1)S(1)} %pad_maximum_fusion) | data formatting | bytes 6389760 | tf_op jit(solution)/shard_map/cond/branch_0_fun/concatenate | solution.py:17
  493.2 13.1 %reshape.197 = bf16[8,2,99840]{2,1,0:T(2,128)(2,1)} reshape(bf16[1024,1,12,130]{3,2,1,0:T(8,128)(2,1)} %bitcast.126) | data formatting | bytes 6389760 | tf_op jit(solution)/shard_map/cond
  506.2 4.0 all-to-all-start
  511.5 36.7 %all-to-all-done = bf16[8,2,99840]{2,1,0:T(2,128)(2,1)S(1)} async-done(((bf16[8,2,99840]{2,1,0:T(2,128)(2,1)}), bf16[8,2,99840]{2,1,0:T(2,128)(2,1)S(1)}, u32[]{:S(2)}, u32[]{:S(2)}) %all-to-all-start) | async-done | bytes 3194912 | tf_op jit(solution)/shard_map/cond/branch_0_fun/all_to_all | solution.py:19
  548.2 10.5 %reshape.198 = bf16[1024,1,12,130]{3,2,1,0:T(8,128)(2,1)} reshape(bf16[8,2,99840]{2,1,0:T(2,128)(2,1)S(1)} %all-to-all-done) | data formatting | bytes 6389760 | tf_op jit(solution)/shard_map/cond
  558.7 7.0 %slice.90 = bf16[8,128,12,128]{3,2,1,0:T(8,128)(2,1)} slice(bf16[8,128,12,130]{3,2,1,0:T(8,128)(2,1)} %bitcast.124), slice={[0:8], [0:128], [0:12], [2:130]} | slice | bytes 6291456 | tf_op jit(solution)/shard_map/cond/branch_0_fun/slice | solution.py:24
  565.6 4.9 fusion.44
  570.6 7.1 %copy.125 = bf16[8,128,12,128]{1,0,3,2:T(8,128)(2,1)S(1)} copy(bf16[8,128,12,128]{3,2,1,0:T(8,128)(2,1)} %slice.90) | data formatting | bytes 6291456 | tf_op jit(solution)/shard_map/cond
  577.7 4.6 copy.126
  582.3 4.6 copy.127
  587.0 2.0 multiply_reduce_fusion
  589.1 4.3 fusion.21
  593.4 2.7 collective-permute-start
  596.1 22.2 %all-gather = bf16[1024,128]{1,0:T(8,128)(2,1)S(1)} all-gather(bf16[64,128]{1,0:T(8,128)(2,1)S(1)} %bitcast.144), channel_id=2, replica_groups=mesh['queue'=16,'tok'=8] {'queue'}, dimensions={0}, use_global_device_ids=true | all-gather | bytes 278528 | tf_op jit(solution)/shard_map/cond/branch_0_fun/all_gather | solution.py:37
  618.3 0.6 dynamic-slice_convert_fusion
  618.9 0.6 select_bitcast_fusion.1
  (71 shorter events, 4.5 us)
Async XLA Ops:
  13.6 7.4 %copy-start.10 = (f32[1536]{0:T(1024)S(1)}, f32[1536]{0:T(1024)}, u32[]{:S(2)}) copy-start(f32[1536]{0:T(1024)} %param.18) | copy-start | bytes 18436
  13.6 7.4 %copy-start.11 = (f32[1536]{0:T(1024)S(1)}, f32[1536]{0:T(1024)}, u32[]{:S(2)}) copy-start(f32[1536]{0:T(1024)} %param.19) | copy-start | bytes 18436
  23.1 2.1 copy-start.2
  25.3 71.4 %copy-start.4 = (bf16[1536,64]{0,1:T(8,128)(2,1)S(1)}, bf16[1536,64]{0,1:T(8,128)(2,1)}, u32[]{:S(2)}) copy-start(bf16[1536,64]{0,1:T(8,128)(2,1)} %param.21) | copy-start | bytes 589828
  25.3 71.4 %copy-start.6 = (f32[1,128,64]{1,2,0:T(8,128)S(1)}, f32[1,128,64]{1,2,0:T(8,128)}, u32[]{:S(2)}) copy-start(f32[1,128,64]{1,2,0:T(8,128)} %param.12) | copy-start | bytes 98308
  95.3 101.0 %copy-start.3 = (f32[64,3,1536]{2,0,1:T(8,128)S(1)}, f32[64,3,1536]{2,0,1:T(8,128)}, u32[]{:S(2)}) copy-start(f32[64,3,1536]{2,0,1:T(8,128)} %param.16) | copy-start | bytes 3538948
  95.3 101.0 %copy-start.5 = (bf16[64,1536]{1,0:T(8,128)(2,1)S(1)}, bf16[64,1536]{1,0:T(8,128)(2,1)}, u32[]{:S(2)}) copy-start(bf16[64,1536]{1,0:T(8,128)(2,1)} %param.15) | copy-start | bytes 589828
  95.3 101.0 %copy-start.13 = (s32[16]{0:T(128)S(1)}, s32[16]{0:T(128)}, u32[]{:S(2)}) copy-start(s32[16]{0:T(128)} %param.13) | copy-start | bytes 196
  100.7 94.9 %collective-permute-start.1 = (bf16[128,64]{0,1:T(8,128)(2,1)S(1)}, bf16[128,64]{0,1:T(8,128)(2,1)S(1)}, u32[]{:S(2)}, u32[]{:S(2)}) collective-permute-start(bf16[128,64]{0,1:T(8,128)(2,1)S(1)} %get-tuple-element.162), channel_id=1, source_target_pairs={{8,0},{16,8},{24,16},{32,24},{40,32},{48,40},{56,48},{64,56},{72,6... | collective-permute-start | bytes 49160 | tf_op jit(solution)/shard_map/ppermute | solution.py:33
  196.3 17.7 %copy-start.7 = (f32[1,128,64]{1,2,0:T(8,128)}, f32[1,128,64]{1,2,0:T(8,128)S(1)}, u32[]{:S(2)}) copy-start(f32[1,128,64]{1,2,0:T(8,128)S(1)} %get-tuple-element.49) | copy-start | bytes 98308 | tf_op jit(solution)/shard_map/cond
  196.3 56.1 %all-gather.7.cloned.1.call-start = ((), (), s32[]{:S(2)}) async-start(), calls=%async_computation.2 | async-start | bytes 3538944 | tf_op jit(solution)/shard_map/cond/branch_0_fun/all_gather | solution.py:122
  210.5 9.7 %copy-start.1 = (f32[128,1536]{1,0:T(8,128)}, f32[128,1536]{1,0:T(8,128)S(1)}, u32[]{:S(2)}) copy-start(f32[128,1536]{1,0:T(8,128)S(1)} %get-tuple-element.148) | copy-start | bytes 2359300 | tf_op jit(solution)/shard_map/cond
  215.0 133.6 %all-gather.5.cloned.1.call-start = ((), (), s32[]{:S(2)}) async-start(), calls=%async_computation.1 | async-start | bytes 13369344 | tf_op jit(solution)/shard_map/cond/branch_0_fun/all_gather | solution.py:128
  506.2 42.0 %all-to-all-start = ((bf16[8,2,99840]{2,1,0:T(2,128)(2,1)}), bf16[8,2,99840]{2,1,0:T(2,128)(2,1)S(1)}, u32[]{:S(2)}, u32[]{:S(2)}) async-start(bf16[8,2,99840]{2,1,0:T(2,128)(2,1)} %reshape.197), calls=%async_computation | async-start | bytes 6389760 | tf_op jit(solution)/shard_map/cond/branch_0_fun/all_to_all | solution.py:19
  558.7 7.0 %copy-start = (bf16[1024,1,12,130]{3,2,1,0:T(8,128)(2,1)S(1)}, bf16[1024,1,12,130]{3,2,1,0:T(8,128)(2,1)}, u32[]{:S(2)}) copy-start(bf16[1024,1,12,130]{3,2,1,0:T(8,128)(2,1)} %reshape.198) | copy-start | bytes 9584644 | tf_op jit(solution)/shard_map/cond
  577.7 11.4 %copy-start.8 = (f32[1,128,64]{1,2,0:T(8,128)S(1)}, f32[1,128,64]{1,2,0:T(8,128)}, u32[]{:S(2)}) copy-start(f32[1,128,64]{1,2,0:T(8,128)} %copy-done.7) | copy-start | bytes 98308 | tf_op jit(solution)/shard_map/cond
  577.7 11.4 %copy-start.12 = (f32[1536]{0:T(1024)S(1)}, f32[1536]{0:T(1024)}, u32[]{:S(2)}) copy-start(f32[1536]{0:T(1024)} %get-tuple-element.142) | copy-start | bytes 18436 | tf_op jit(solution)/shard_map/cond
  586.9 31.9 %copy-start.9 = (f32[128,64]{0,1:T(8,128)S(1)}, f32[128,64]{0,1:T(8,128)}, u32[]{:S(2)}) copy-start(f32[128,64]{0,1:T(8,128)} %get-tuple-element.58) | copy-start | bytes 98308 | tf_op jit(solution)/shard_map/cond
  593.4 25.5 %collective-permute-start = (bf16[128,64]{0,1:T(8,128)(2,1)S(1)}, bf16[128,64]{0,1:T(8,128)(2,1)S(1)}, u32[]{:S(2)}, u32[]{:S(2)}) collective-permute-start(bf16[128,64]{0,1:T(8,128)(2,1)S(1)} %get-tuple-element.153), channel_id=1, source_target_pairs={{8,0},{16,8},{24,16},{32,24},{40,32},{48,40},{56,48},{64,56},{72,6... | collective-permute-start | bytes 49160 | tf_op jit(solution)/shard_map/cond/branch_0_fun/ppermute | solution.py:33
Sparse Core Ops, SparseCore 0:
  215.1 37.2 all-gather.6
  254.8 93.6 all-gather.4

commit v2 on v1

--- a/solution.py
+++ b/solution.py
@@ -167,9 +167,14 @@
     return lax.dot_general(a, b, (((1,), (1,)), ((), ())), preferred_element_type=jnp.float32)
 
 
-def attention_kernel(q_in, kv_in, out, q_all, kv_all, o_send, o_recv, a_send,
-                     xq_s, xq_r, xk_s, xk_r, yq_s, yq_r, zk_s, zk_r, ck_s, ck_r,
-                     oy_s, oy_r, ox_s, ox_r):
+def block_kernel(latent_in, mod_in, coef_in, patch_in, qkv_hbm, q_gain_in, k_gain_in, out_hbm,
+                 head_hbm, tail_hbm, vel_out, next_out, leaving_out, wide_out,
+                 q_in, kv_in, q_all, kv_all, o_send, o_recv, a_send, out,
+                 w_buf, ow_buf, hw_buf, tail_buf, hidden_buf, normed_buf, proj_buf,
+                 size_buf, u_send, u_recv, lv_send, lv_recv,
+                 w_sem, ow_sem, hw_sem, tail_sem, f_s, f_r, u_s, u_r, lv_s, lv_r,
+                 xq_s, xq_r, xk_s, xk_r, yq_s, yq_r, zk_s, zk_r, ck_s, ck_r,
+                 oy_s, oy_r, ox_s, ox_r):
     queue = lax.axis_index("queue")
     tok = lax.axis_index("tok")
     core = lax.rem(queue, 2)
@@ -257,24 +262,114 @@
         return remote(a_send.at[h, g], out.at[g * 3 + h], ox_s.at[h, d], ox_r.at[h, d],
                       device(g, y, z, core))
 
+    def size_step(stage, d, arriving=False):
+        if stage == 0:
+            dev, src = device(hop(x, d), y, z, core), device(hop(x, -d), y, z, core)
+        elif stage == 1:
+            dev, src = device(x, y, hop(z, d), core), device(x, y, hop(z, -d), core)
+        elif stage == 2:
+            dev, src = device(x, hop(y, d), z, core), device(x, hop(y, -d), z, core)
+        else:
+            dev, src = device(x, y, z, 1 - core), device(x, y, z, 1 - core)
+        return remote(size_buf.at[stage, 0], size_buf.at[stage, d],
+                      f_s.at[stage, d], f_r.at[stage, d], src if arriving else dev)
+
+    def size_peers(stage):
+        return (1, 2, 3) if stage < 3 else (1,)
+
+    def size_send(stage):
+        for d in size_peers(stage):
+            size_step(stage, d).start()
+
+    def size_take(stage):
+        top = size_buf[stage, 0]
+        for d in size_peers(stage):
+            size_step(stage, d, True).wait_recv()
+            top = jnp.maximum(top, size_buf[stage, d])
+        return top
+
+    def weight(b):
+        return pltpu.make_async_copy(qkv_hbm.at[:, b * 512:(b + 1) * 512], w_buf.at[b],
+                                     w_sem.at[b])
+
+    out_copy = pltpu.make_async_copy(out_hbm, ow_buf, ow_sem)
+    head_copy = pltpu.make_async_copy(head_hbm, hw_buf, hw_sem)
+    tail_copy = pltpu.make_async_copy(tail_hbm, tail_buf, tail_sem)
+    for b in (3, 4, 5, 6, 7, 8, 0, 1, 2):
+        weight(b).start()
     barrier = pltpu.get_barrier_semaphore()
+    for n in range(1, 16):
+        pl.semaphore_signal(barrier, inc=1, device_id=(lax.rem(queue + n, 16), tok),
+                            device_id_type=MESH_ID)
+    for d in (1, 3):
+        pl.semaphore_signal(barrier, inc=1, device_id=device(hop(x, d), y, z, core),
+                            device_id_type=MESH_ID)
     for d in (1, 2, 3):
-        for dev in (device(hop(x, d), y, z, core), device(x, hop(y, d), z, core),
-                    device(x, y, hop(z, d), core)):
-            pl.semaphore_signal(barrier, inc=1, device_id=dev, device_id_type=MESH_ID)
-    pl.semaphore_signal(barrier, inc=1, device_id=device(x, y, z, 1 - core),
-                        device_id_type=MESH_ID)
-    pl.semaphore_wait(barrier, 10)
-
+        pl.semaphore_signal(barrier, inc=1, device_id=device(x, hop(y, d), z, core),
+                            device_id_type=MESH_ID)
+
+    hidden = jnp.dot(latent_in[...].astype(jnp.bfloat16), patch_in[...],
+                     preferred_element_type=jnp.float32)
+    hidden_buf[...] = hidden
+    normed_buf[...] = (layer_norm(hidden) * (1.0 + mod_in[1:2, :]) + mod_in[0:1, :]).astype(
+        jnp.bfloat16)
+
+    def project(b, at):
+        weight(b).wait()
+        part = jnp.dot(normed_buf[...], w_buf[b], preferred_element_type=jnp.float32)
+        proj_buf[:, at * 512:(at + 1) * 512] = part
+        return jnp.sum(part * part, axis=-1, keepdims=True)
+
+    def pick():
+        row = lax.broadcasted_iota(jnp.int32, (1536, 128), 0)
+        lane = lax.broadcasted_iota(jnp.int32, (1536, 128), 1)
+        return jnp.logical_and(row >= lane * 128, row < lane * 128 + 128).astype(jnp.bfloat16)
+
+    def top_norm(values):
+        wide = values.astype(jnp.float32)
+        sums = jnp.dot((wide * wide).astype(jnp.bfloat16), pick(),
+                       preferred_element_type=jnp.float32)
+        return jnp.max(sums, axis=0, keepdims=True) * 1.01
+
+    square = project(3, 0) + project(4, 1) + project(5, 2)
+    factor = lax.rsqrt(square * (1.0 / 1536) + 1e-06)
+    keys = (proj_buf[...] * factor * k_gain_in[...]).astype(jnp.bfloat16)
+    for n in range(12):
+        kv_in[n, 0] = keys[:, n * 128:(n + 1) * 128]
+    key_size = top_norm(keys)
+    top = jnp.zeros((128, 128), jnp.float32)
+    for b in range(3):
+        weight(6 + b).wait()
+        part = jnp.dot(normed_buf[...], w_buf[6 + b], preferred_element_type=jnp.float32)
+        part = part * VALUE_SHRINK
+        for n in range(4):
+            piece = part[:, n * 128:(n + 1) * 128]
+            top = jnp.maximum(top, jnp.abs(piece))
+            kv_in[b * 4 + n, 1] = piece.astype(jnp.bfloat16)
+    value_size = jnp.max(top, axis=0, keepdims=True)
+
+    pl.semaphore_wait(barrier, 20)
     for h in range(3):
         for d in (1, 3, 2):
             x_keys(h, d).start()
-        for d in (1, 3, 2):
-            x_query(h, d).start()
-    for h in range(3):
-        q_all[h, y, rows(x, 128), :] = q_in[x * 3 + h]
         for kv in range(2):
             kv_all[h, kv, rows(slot * 4 + x, 128), :] = kv_in[x * 3 + h, kv]
+
+    square = project(0, 0) + project(1, 1) + project(2, 2)
+    out_copy.start()
+    head_copy.start()
+    tail_copy.start()
+    factor = lax.rsqrt(square * (1.0 / 1536) + 1e-06) * (HEAD_DIM ** (-0.5) * LOG2E)
+    queries = (proj_buf[...] * factor * q_gain_in[...]).astype(jnp.bfloat16)
+    for n in range(12):
+        q_in[n] = queries[:, n * 128:(n + 1) * 128]
+    for h in range(3):
+        for d in (1, 3, 2):
+            x_query(h, d).start()
+        q_all[h, y, rows(x, 128), :] = q_in[x * 3 + h]
+    size_buf[0, 0] = jnp.concatenate(
+        [top_norm(queries), key_size, value_size, jnp.zeros((5, 128), jnp.float32)], axis=0)
+    size_send(0)
 
     def spread(h):
         for d in (1, 3, 2):
@@ -363,13 +458,76 @@
         def _():
             combine(h - 1)
 
+        for stage in range(3):
+            @pl.when(t == 2 * stage + 2)
+            def _():
+                size_buf[stage + 1, 0] = size_take(stage)
+                size_send(stage + 1)
+
         return carry
 
     lax.fori_loop(0, 12, chunk, 0)
+    sizes = size_take(3)
+    wide = jnp.maximum(sizes[0:1] * sizes[1:2] - SAFE_LOG2 * SAFE_LOG2, sizes[2:3] - 2.0)
+    wide = jnp.max(wide, axis=1, keepdims=True)
+    wide_out[...] = jnp.broadcast_to(wide, (8, 128))
     combine(2)
+    out_copy.wait()
+    head_copy.wait()
+    tail_copy.wait()
     for h in range(3):
         for d in (1, 3, 2):
             x_back_in(h, d).wait_recv()
+    attended = jnp.concatenate([out[n] for n in range(12)], axis=1)
+    attn_out = jnp.dot(attended, ow_buf[...], preferred_element_type=jnp.float32)
+    residual = hidden_buf[...] + mod_in[2:3, :] * attn_out
+    velocity = jnp.dot(residual.astype(jnp.bfloat16), hw_buf[...],
+                       preferred_element_type=jnp.float32)
+    vel_out[...] = velocity
+    updated = jnp.transpose(latent_in[...] + coef_in[0] * velocity)
+    u_send[...] = updated
+
+    send_next = remote(u_send, u_recv, u_s, u_r, (lax.rem(queue + 15, 16), tok))
+    take_next = remote(u_send, u_recv, u_s, u_r, (lax.rem(queue + 1, 16), tok))
+
+    def send_leaving(n):
+        return remote(lv_send.at[n], lv_recv, lv_s.at[n], lv_r, (n, tok))
+
+    @pl.when(queue > 0)
+    def _():
+        send_next.start()
+
+    @pl.when(queue == 0)
+    def _():
+        for n in range(1, 16):
+            lv_send[n, 0:4, :] = updated[n * 4:n * 4 + 4, :]
+            lv_send[n, 4:8, :] = jnp.zeros((4, 128), jnp.float32)
+            send_leaving(n).start()
+        leaving_out[...] = updated[0:4, :]
+
+    @pl.when(queue == 15)
+    def _():
+        next_out[...] = tail_buf[...]
+
+    @pl.when(queue < 15)
+    def _():
+        take_next.wait_recv()
+        next_out[...] = jnp.transpose(u_recv[...])
+
+    @pl.when(queue > 0)
+    def _():
+        send_leaving(0).wait_recv()
+        leaving_out[...] = lv_recv[0:4, :]
+        send_next.wait_send()
+
+    @pl.when(queue == 0)
+    def _():
+        for n in range(1, 16):
+            send_leaving(n).wait_send()
+
+    for stage in range(4):
+        for d in size_peers(stage):
+            size_step(stage, d).wait_send()
     for h in range(3):
         for d in (1, 2, 3):
             x_keys(h, d).wait_send()
@@ -382,25 +540,50 @@
             c_keys(h, d).wait_send()
 
 
-def attention(q_in, kv_in):
+def block(*operands):
     sems = [pltpu.SemaphoreType.DMA((3, 4))] * 14
+    vmem, hbm = pl.BlockSpec(memory_space=pltpu.VMEM), pl.BlockSpec(memory_space=pltpu.HBM)
+    smem = pl.BlockSpec(memory_space=pltpu.SMEM)
+    f32, bf16, dma = jnp.float32, jnp.bfloat16, pltpu.SemaphoreType.DMA
     return pl.pallas_call(
-        attention_kernel,
-        out_shape=jax.ShapeDtypeStruct((12, 128, 128), jnp.bfloat16),
-        in_specs=[pl.BlockSpec(memory_space=pltpu.VMEM)] * 2,
-        out_specs=pl.BlockSpec(memory_space=pltpu.VMEM),
+        block_kernel,
+        out_shape=[
+            jax.ShapeDtypeStruct((128, 64), f32),
+            jax.ShapeDtypeStruct((128, 64), f32),
+            jax.ShapeDtypeStruct((4, 128), f32),
+            jax.ShapeDtypeStruct((8, 128), f32),
+        ],
+        in_specs=[vmem, vmem, smem, vmem, hbm, vmem, vmem, hbm, hbm, hbm],
+        out_specs=[vmem] * 4,
         scratch_shapes=[
-            pltpu.VMEM((3, 4, 512, 128), jnp.bfloat16),
-            pltpu.VMEM((3, 2, 4096, 128), jnp.bfloat16),
-            pltpu.VMEM((3, 4, 528, 128), jnp.bfloat16),
-            pltpu.VMEM((3, 4, 528, 128), jnp.bfloat16),
-            pltpu.VMEM((3, 4, 128, 128), jnp.bfloat16),
+            pltpu.VMEM((12, 128, 128), bf16),
+            pltpu.VMEM((12, 2, 128, 128), bf16),
+            pltpu.VMEM((3, 4, 512, 128), bf16),
+            pltpu.VMEM((3, 2, 4096, 128), bf16),
+            pltpu.VMEM((3, 4, 528, 128), bf16),
+            pltpu.VMEM((3, 4, 528, 128), bf16),
+            pltpu.VMEM((3, 4, 128, 128), bf16),
+            pltpu.VMEM((12, 128, 128), bf16),
+            pltpu.VMEM((9, 1536, 512), bf16),
+            pltpu.VMEM((1536, 1536), bf16),
+            pltpu.VMEM((1536, 64), bf16),
+            pltpu.VMEM((128, 64), f32),
+            pltpu.VMEM((128, 1536), f32),
+            pltpu.VMEM((128, 1536), bf16),
+            pltpu.VMEM((128, 1536), f32),
+            pltpu.VMEM((4, 4, 8, 128), f32),
+            pltpu.VMEM((64, 128), f32),
+            pltpu.VMEM((64, 128), f32),
+            pltpu.VMEM((16, 8, 128), f32),
+            pltpu.VMEM((8, 128), f32),
+            dma((9,)), dma(()), dma(()), dma(()), dma((4, 4)), dma((4, 4)),
+            dma(()), dma(()), dma((16,)), dma(()),
         ] + sems,
         compiler_params=pltpu.CompilerParams(
-            collective_id=1, has_side_effects=True, vmem_limit_bytes=56 * 2**20),
-        cost_estimate=pl.CostEstimate(flops=13 * 10**9, bytes_accessed=20 * 10**6,
+            collective_id=1, has_side_effects=True, vmem_limit_bytes=58 * 2**20),
+        cost_estimate=pl.CostEstimate(flops=16 * 10**9, bytes_accessed=40 * 10**6,
                                       transcendentals=25 * 10**6),
-    )(q_in, kv_in)
+    )(*operands)
 
 
 def per_device(
@@ -415,55 +598,20 @@
     out_weight,
     head_weight,
 ):
-    feature = patch_weight.shape[1]
-    heads = feature // HEAD_DIM
     levels = time_table.shape[0]
-    frames = lax.axis_size("queue")
     position = lax.axis_index("queue")
-    latent = latents[0]
     level_now = step_index[position]
     level_before = jnp.where(position > 0, step_index[jnp.maximum(position - 1, 0)], -1)
     modulation = lax.dynamic_index_in_dim(time_table, level_now, 0, keepdims=False)
-    hidden = jnp.dot(latent.astype(jnp.bfloat16), patch_weight, preferred_element_type=jnp.float32)
-    normed = (layer_norm(hidden) * (1.0 + modulation[1]) + modulation[0]).astype(jnp.bfloat16)
-    projected = jnp.dot(normed, qkv_weight, preferred_element_type=jnp.float32)
-    scale = HEAD_DIM ** (-0.5) * LOG2E
-    queries = (rms_norm(projected[:, :feature], q_gain) * scale).astype(jnp.bfloat16)
-    keys = rms_norm(projected[:, feature:2 * feature], k_gain).astype(jnp.bfloat16)
-    values = (projected[:, 2 * feature:] * VALUE_SHRINK).astype(jnp.bfloat16)
-
-    def by_head(a):
-        return a.reshape(-1, heads, HEAD_DIM).transpose(1, 0, 2)
-
-    q_heads, k_heads, v_heads = by_head(queries), by_head(keys), by_head(values)
-
-    def top_norm(a):
-        wide = a.astype(jnp.float32)
-        return jnp.max(jnp.sum(wide * wide, axis=-1), axis=-1)
-
-    sizes = jnp.stack([top_norm(q_heads), top_norm(k_heads),
-                       jnp.max(jnp.abs(v_heads.astype(jnp.float32)), axis=(1, 2))])
-    sizes = lax.pmax(sizes, ("queue", "tok"))
-    plain = jnp.logical_and(jnp.all(jnp.sqrt(sizes[0]) * jnp.sqrt(sizes[1]) <= SAFE_LOG2),
-                            jnp.all(sizes[2] <= 2.0))
-    attended = attention(q_heads, jnp.stack([k_heads, v_heads], axis=1))
-    attended = attended.transpose(1, 0, 2).reshape(-1, feature)
-    attn_out = jnp.dot(attended, out_weight, preferred_element_type=jnp.float32)
-    residual = hidden + modulation[2] * attn_out
-    velocity = jnp.dot(
-        residual.astype(jnp.bfloat16), head_weight, preferred_element_type=jnp.float32
-    )
     sigma_now = (level_now.astype(jnp.float32) + 1.0) / levels
     sigma_next = (level_before.astype(jnp.float32) + 1.0) / levels
-    updated = latent + (sigma_next - sigma_now) * velocity
-    arrived = passed_along(updated.astype(jnp.bfloat16), "queue", -1).astype(updated.dtype)
-    queue_next = jnp.where(position == frames - 1, tail_noise, arrived)
-    clean_frame = picked(updated.T.astype(jnp.bfloat16), "queue", 0).astype(jnp.float32)
-    channel_share = clean_frame.shape[0] // frames
-    leaving = lax.dynamic_slice_in_dim(clean_frame, position * channel_share, channel_share, 0)
+    velocity, queue_next, leaving, wide = block(
+        latents[0], modulation, (sigma_next - sigma_now)[None], patch_weight, qkv_weight,
+        q_gain[None], k_gain[None], out_weight, head_weight, tail_noise)
     args = (latents, step_index, tail_noise, patch_weight, time_table, qkv_weight, q_gain,
             k_gain, out_weight, head_weight)
-    return lax.cond(plain, lambda *_: (velocity[None], queue_next[None], leaving), careful, *args)
+    return lax.cond(wide[0, 0] <= 0.0, lambda *_: (velocity[None], queue_next[None], leaving),
+                    careful, *args)
 
 
 def solution(mesh):

time: 636 us -> 538 us (0.85)
  blocking collectives: 111 us -> 22.2 us
  local copies, waits for them, and re-layouts: 95.1 us -> 113 us
  starting transfers between devices: 22.5 us -> 6.79 us
  matrix products: 98.7 us -> 85.5 us
  Pallas kernels: 70 us -> 81 us
    pmax x1 -> x0, blocking collectives: 64 us -> none  [per_device(): sizes = lax.pmax(sizes, ('queue', 'tok'))]
    all_gather x2 -> x1, blocking collectives: 46.7 us -> 22.2 us  [picked(): lax.all_gather(value, axis)]
    dot_general x3 -> x0, matrix products: 12.5 us -> none  [the longest x1 7.14 us: per_device(): projected = jnp.dot(normed, qkv_weight, preferred_element_type=jnp.float32)]
    all_gather x1, starting transfers between devices: 11.3 us -> 0.04 us  [careful(): whole_queries = lax.all_gather(queries, 'tok', axis=0, tiled=True)]
    pallas_call x1, Pallas kernels: 70 us -> 81 us  [block(): pl.pallas_call(block_kernel, out_shape=[jax.ShapeDtypeStruct((128, 64), f...]
    all_gather x1, waiting for transfers between devices: 93 us -> 84.2 us  [careful(): lax.all_gather(key_value, 'queue', axis=0, tiled=True)]
    all_gather x1, local copies, waits for them, and re-layouts: 3.18 us -> 12 us  [careful(): whole_queries = lax.all_gather(queries, 'tok', axis=0, tiled=True)]
    unnamed x16 -> x23, local copies, waits for them, and re-layouts: 0.04 us -> 6.71 us
  transfers between devices with their start and end apart: 5 -> 4, of which waited for: 3 -> 3; matrix products, arithmetic and copies ran while one was open for 2% -> 4% of each run, Pallas kernels for 0% -> 0%
where the time goes in v2:
time: 538 us; the launch traced here: 528 us
  waiting for transfers between devices  157 us (29%)
  local copies, waits for them, and re-layouts  113 us (21%)
  matrix products  85.5 us (16%)
  Pallas kernels  81 us (15%)
  other arithmetic  43 us (8%)
  blocking collectives  22.2 us (4%)
  between operations  18.5 us (3%)
  starting transfers between devices  6.79 us (1%)
    all_gather x1, waiting for transfers between devices, careful(): lax.all_gather(key_value, 'queue', axis=0, tiled=True)  84.2 us
    pallas_call x1, Pallas kernels, block(): pl.pallas_call(block_kernel, out_shape=[jax.ShapeDtypeStruct((128, 64), f...  81 us
    cond x18, local copies, waits for them, and re-layouts  39.9 us
    dot_general x1, matrix products, fold_keys(): jnp.einsum('rhd,khd->rhk', queries, key_rows, preferred_element_type=jnp....  37 us
    all_to_all x1, waiting for transfers between devices, sent_together(): lax.all_to_all(both, axis, split_axis=split_dim, concat_axis=concat_dim,...  36.8 us
    all_gather x1, waiting for transfers between devices, careful(): whole_queries = lax.all_gather(queries, 'tok', axis=0, tiled=True)  35.7 us
    dot_general x1, matrix products, fold_keys(): jnp.einsum('rhk,khd->rhd', weights.astype(jnp.bfloat16), value_rows, pref...  34.9 us
    reduce_sum x1, other arithmetic, fold_keys(): run_sum = jnp.sum(weights, axis=-1)  31 us
  transfers between devices with their start and end apart: 4, of which 3 were waited for; matrix products, arithmetic and copies ran while one was open for 4% of the time, Pallas kernels for 0%

profile of v2, /device:TPU:1, one launch (start us, length us, event | category | flops | bytes accessed | tf_op | source)
XLA Modules:
  0.0 527.8 jit_solution(15921332148616558766)
XLA Ops:
  7.2 1.5 copy.91
  8.6 1.3 fusion.34
  11.9 0.9 constant_dynamic-slice_fusion
  12.8 0.6 copy.110
  14.8 1.3 broadcast_in_dim.53.q_gain_in
  16.1 1.3 broadcast_in_dim.54.k_gain_in
  17.3 1.8 copy.92.head_hbm
  19.2 1.5 copy.93.tail_hbm
  20.7 81.0 %shard_map.127 = (f32[128,64]{1,0:T(8,128)}, f32[128,64]{1,0:T(8,128)}, f32[4,128]{1,0:T(4,128)}, f32[8,128]{1,0:T(8,128)}) custom-call(f32[128,64]{1,0:T(8,128)} %bitcast.98, f32[3,1536]{1,0:T(4,128)} %bitcast.102, f32[1]{0:T(128)} %bitcast.25.coef_in, bf16[64,1536]{1,0:T(8,128)(2,1)} %patch_in.1, bf16[1536,4608]{1,0:T(8,128)(2,1)} %qkv_hbm.1, ...), custom_call_target="tpu_custom_call" | custom-call | flops 16000000000 | bytes 40000000 | tf_op jit(solution)/shard_map/pallas_call | solution.py:548
  101.7 1.2 slice.44
  103.6 415.6 %conditional.1 = (f32[1,128,64]{1,2,0:T(8,128)S(1)}, f32[1,128,64]{1,2,0:T(8,128)S(1)}, f32[4,128]{1,0:T(4,128)}) conditional(s32[]{:T(128)} %bitcast.26, (f32[1,128,64]{1,2,0:T(8,128)S(1)}, bf16[64,1536]{1,0:T(8,128)(2,1)S(1)}, s32[16]{0:T(128)S(1)}, f32[64,3,1536]{2,0,1:T(8,128)S(1)}, bf16[1536,4608]{1,0:T(8,128)(2,1)}, ...), branch_computations={%region_0.10_spmd, %region_10.11_spmd} | conditional | flops 15579123712 | bytes 533929024 | solution.py:613
  103.8 0.6 fusion.32
  104.4 1.1 convolution_reduce_fusion
  105.5 0.6 fusion.31
  106.1 0.4 fusion.33
  106.4 0.2 multiply_reduce_fusion.3
  106.7 3.3 multiply_reduce_fusion.1
  110.0 0.9 multiply_convert_fusion
  111.0 5.2 fusion.5
  116.2 0.1 multiply_reduce_fusion.2
  116.3 0.1 multiply_convert_fusion.1
  116.5 1.0 pad_maximum_fusion.1
  117.5 35.7 %all-gather.6.cloned.1.call-done = bf16[1024,1536]{1,0:T(8,128)(2,1)} async-done(((bf16[128,1536]{1,0:T(8,128)(2,1)}), bf16[1024,1536]{1,0:T(8,128)(2,1)}) %all-gather.6.cloned.1.call-update) | async-done | bytes 3145744 | tf_op jit(solution)/shard_map/cond/branch_0_fun/all_gather | solution.py:122
  153.2 12.0 %copy.82 = bf16[1024,1536]{0,1:T(8,128)(2,1)S(1)} copy(bf16[1024,1536]{1,0:T(8,128)(2,1)} %all-gather.6.cloned.1.call-done) | data formatting | bytes 6291456 | tf_op jit(solution)/shard_map/cond/branch_0_fun/all_gather | solution.py:122
  165.2 84.2 %all-gather.4.cloned.1.call-done = bf16[2048,3072]{1,0:T(8,128)(2,1)} async-done(((bf16[128,3072]{1,0:T(8,128)(2,1)}), bf16[2048,3072]{1,0:T(8,128)(2,1)}) %all-gather.4.cloned.1.call-update) | async-done | bytes 12582928 | tf_op jit(solution)/shard_map/cond/branch_0_fun/all_gather | solution.py:128
  249.3 10.2 %fusion.29 = (bf16[2048,1536]{1,0:T(8,128)(2,1)}, bf16[2048,1536]{1,0:T(8,128)(2,1)}) fusion(bf16[2048,3072]{1,0:T(8,128)(2,1)} %all-gather.4.cloned.1.call-done), kind=kLoop, calls=%fused_computation.58 | loop fusion | bytes 25165824 | tf_op jit(solution)/shard_map/cond/branch_0_fun/slice | solution.py:56
  259.5 8.7 %copy.81 = bf16[2048,1536]{0,1:T(8,128)(2,1)} copy(bf16[2048,1536]{1,0:T(8,128)(2,1)} %get-tuple-element.118) | data formatting | bytes 12582912 | tf_op jit(solution)/shard_map/cond/branch_0_fun/slice | solution.py:56
  268.2 37.0 %bitcast_reduce_fusion = (f32[1024,12]{0,1:T(8,128)S(1)}, f32[12,2048,1024]{2,1,0:T(8,128)}) fusion(bf16[2048,12,128]{0,2,1:T(8,128)(2,1)} %bitcast.90, bf16[1024,12,128]{0,2,1:T(8,128)(2,1)S(1)} %bitcast.92), kind=kOutput, calls=%fused_computation.1 | convolution fusion | flops 6492770304 | bytes 110149632 | tf_op jit(solution)/shard_map/cond/branch_0_fun/rhd,khd->rhk/dot_general | solution.py:59
  305.2 8.7 %copy.85 = bf16[2048,1536]{0,1:T(8,128)(2,1)} copy(bf16[2048,1536]{1,0:T(8,128)(2,1)} %get-tuple-element.119) | data formatting | bytes 12582912 | tf_op jit(solution)/shard_map/cond/branch_0_fun/slice | solution.py:57
  313.9 31.0 %fusion.2 = bf16[1024,12]{0,1:T(8,128)(2,1)S(1)} fusion(f32[12,2048,1024]{2,1,0:T(8,128)} %get-tuple-element.133, f32[1024,12]{0,1:T(8,128)S(1)} %broadcast_maximum_fusion), kind=kLoop, calls=%fused_computation.4 | loop fusion | flops 75485184 | bytes 100737024 | tf_op jit(solution)/shard_map/cond/branch_0_fun/reduce_sum | solution.py:63
  345.0 34.9 %convert_bitcast_fusion = bf16[1,1024,12,128]{1,3,2,0:T(8,128)(2,1)S(1)} fusion(bf16[2048,12,128]{0,2,1:T(8,128)(2,1)} %bitcast.91, f32[12,2048,1024]{2,1,0:T(8,128)} %get-tuple-element.133, f32[1024,12]{0,1:T(8,128)S(1)} %broadcast_maximum_fusion), kind=kOutput, calls=%fused_computation.12 | convolution fusion | flops 6519521280 | bytes 110149632 | tf_op jit(solution)/shard_map/cond/branch_0_fun/rhk,khd->rhd/dot_general | solution.py:64
  380.0 1.2 pad_maximum_fusion
  381.2 12.6 %copy.89 = bf16[1,1024,12,130]{3,2,0,1:T(8,128)(2,1)} copy(bf16[1,1024,12,130]{1,3,2,0:T(8,128)(2,1)S(1)} %pad_maximum_fusion) | data formatting | bytes 6389760 | tf_op jit(solution)/shard_map/cond/branch_0_fun/concatenate | solution.py:17
  393.9 13.0 %reshape.130 = bf16[8,2,99840]{2,1,0:T(2,128)(2,1)} reshape(bf16[1024,1,12,130]{3,2,1,0:T(8,128)(2,1)} %bitcast.89) | data formatting | bytes 6389760 | tf_op jit(solution)/shard_map/cond
  406.9 4.0 all-to-all-start
  412.1 36.8 %all-to-all-done = bf16[8,2,99840]{2,1,0:T(2,128)(2,1)S(1)} async-done(((bf16[8,2,99840]{2,1,0:T(2,128)(2,1)}), bf16[8,2,99840]{2,1,0:T(2,128)(2,1)S(1)}, u32[]{:S(2)}, u32[]{:S(2)}) %all-to-all-start) | async-done | bytes 3194912 | tf_op jit(solution)/shard_map/cond/branch_0_fun/all_to_all | solution.py:19
  448.9 10.5 %reshape.131 = bf16[1024,1,12,130]{3,2,1,0:T(8,128)(2,1)} reshape(bf16[8,2,99840]{2,1,0:T(2,128)(2,1)S(1)} %all-to-all-done) | data formatting | bytes 6389760 | tf_op jit(solution)/shard_map/cond
  459.4 6.9 %slice.53 = bf16[8,128,12,128]{3,2,1,0:T(8,128)(2,1)} slice(bf16[8,128,12,130]{3,2,1,0:T(8,128)(2,1)} %bitcast.87), slice={[0:8], [0:128], [0:12], [2:130]} | slice | bytes 6291456 | tf_op jit(solution)/shard_map/cond/branch_0_fun/slice | solution.py:24
  466.3 5.0 fusion.30
  471.3 7.1 %copy.103 = bf16[8,128,12,128]{1,0,3,2:T(8,128)(2,1)S(1)} copy(bf16[8,128,12,128]{3,2,1,0:T(8,128)(2,1)} %slice.53) | data formatting | bytes 6291456 | tf_op jit(solution)/shard_map/cond
  478.4 4.6 copy.104
  483.1 4.6 copy.105
  487.7 2.0 multiply_reduce_fusion
  489.9 3.6 fusion.21
  493.5 2.7 collective-permute-start
  496.2 22.2 %all-gather = bf16[1024,128]{1,0:T(8,128)(2,1)S(1)} all-gather(bf16[64,128]{1,0:T(8,128)(2,1)S(1)} %bitcast.97), channel_id=2, replica_groups=mesh['queue'=16,'tok'=8] {'queue'}, dimensions={0}, use_global_device_ids=true | all-gather | bytes 278528 | tf_op jit(solution)/shard_map/cond/branch_0_fun/all_gather | solution.py:37
  518.4 0.6 dynamic-slice_convert_fusion
  519.3 1.2 copy.118
  (52 shorter events, 0.6 us)
Async XLA Ops:
  20.7 82.9 %copy-start.2 = (f32[64,3,1536]{2,0,1:T(8,128)S(1)}, f32[64,3,1536]{2,0,1:T(8,128)}, u32[]{:S(2)}) copy-start(f32[64,3,1536]{2,0,1:T(8,128)} %param.16) | copy-start | bytes 3538948
  20.7 82.9 %copy-start.3 = (bf16[1536,64]{0,1:T(8,128)(2,1)S(1)}, bf16[1536,64]{0,1:T(8,128)(2,1)}, u32[]{:S(2)}) copy-start(bf16[1536,64]{0,1:T(8,128)(2,1)} %param.21) | copy-start | bytes 589828
  20.7 82.9 %copy-start.4 = (f32[1,128,64]{1,2,0:T(8,128)S(1)}, f32[1,128,64]{1,2,0:T(8,128)}, u32[]{:S(2)}) copy-start(f32[1,128,64]{1,2,0:T(8,128)} %param.12) | copy-start | bytes 98308
  20.7 82.9 %copy-start.7 = (bf16[64,1536]{1,0:T(8,128)(2,1)S(1)}, bf16[64,1536]{1,0:T(8,128)(2,1)}, u32[]{:S(2)}) copy-start(bf16[64,1536]{1,0:T(8,128)(2,1)} %patch_in.1) | copy-start | bytes 589828
  20.7 82.9 %copy-start.10 = (f32[1536]{0:T(1024)S(1)}, f32[1536]{0:T(1024)}, u32[]{:S(2)}) copy-start(f32[1536]{0:T(1024)} %param.18) | copy-start | bytes 18436
  20.7 82.9 %copy-start.11 = (f32[1536]{0:T(1024)S(1)}, f32[1536]{0:T(1024)}, u32[]{:S(2)}) copy-start(f32[1536]{0:T(1024)} %param.19) | copy-start | bytes 18436
  20.7 82.9 %copy-start.14 = (s32[16]{0:T(128)S(1)}, s32[16]{0:T(128)}, u32[]{:S(2)}) copy-start(s32[16]{0:T(128)} %param.13) | copy-start | bytes 196
  103.6 6.3 %copy-start.5 = (f32[1,128,64]{1,2,0:T(8,128)}, f32[1,128,64]{1,2,0:T(8,128)S(1)}, u32[]{:S(2)}) copy-start(f32[1,128,64]{1,2,0:T(8,128)S(1)} %get-tuple-element.26) | copy-start | bytes 98308 | tf_op jit(solution)/shard_map/cond
  103.6 49.5 %all-gather.6.cloned.1.call-start = ((), (), s32[]{:S(2)}) async-start(), calls=%async_computation.2 | async-start | bytes 3538944 | tf_op jit(solution)/shard_map/cond/branch_0_fun/all_gather | solution.py:122
  106.4 9.7 %copy-start.1 = (f32[128,1536]{1,0:T(8,128)}, f32[128,1536]{1,0:T(8,128)S(1)}, u32[]{:S(2)}) copy-start(f32[128,1536]{1,0:T(8,128)S(1)} %get-tuple-element.129) | copy-start | bytes 2359300 | tf_op jit(solution)/shard_map/cond
  110.9 138.4 %all-gather.4.cloned.1.call-start = ((), (), s32[]{:S(2)}) async-start(), calls=%async_computation.1 | async-start | bytes 13369344 | tf_op jit(solution)/shard_map/cond/branch_0_fun/all_gather | solution.py:128
  406.9 42.0 %all-to-all-start = ((bf16[8,2,99840]{2,1,0:T(2,128)(2,1)}), bf16[8,2,99840]{2,1,0:T(2,128)(2,1)S(1)}, u32[]{:S(2)}, u32[]{:S(2)}) async-start(bf16[8,2,99840]{2,1,0:T(2,128)(2,1)} %reshape.130), calls=%async_computation | async-start | bytes 6389760 | tf_op jit(solution)/shard_map/cond/branch_0_fun/all_to_all | solution.py:19
  459.4 7.0 %copy-start = (bf16[1024,1,12,130]{3,2,1,0:T(8,128)(2,1)S(1)}, bf16[1024,1,12,130]{3,2,1,0:T(8,128)(2,1)}, u32[]{:S(2)}) copy-start(bf16[1024,1,12,130]{3,2,1,0:T(8,128)(2,1)} %reshape.131) | copy-start | bytes 9584644 | tf_op jit(solution)/shard_map/cond
  478.4 11.4 %copy-start.6 = (f32[1,128,64]{1,2,0:T(8,128)S(1)}, f32[1,128,64]{1,2,0:T(8,128)}, u32[]{:S(2)}) copy-start(f32[1,128,64]{1,2,0:T(8,128)} %copy-done.5) | copy-start | bytes 98308 | tf_op jit(solution)/shard_map/cond
  478.4 11.4 %copy-start.12 = (f32[1536]{0:T(1024)S(1)}, f32[1536]{0:T(1024)}, u32[]{:S(2)}) copy-start(f32[1536]{0:T(1024)} %get-tuple-element.123) | copy-start | bytes 18436 | tf_op jit(solution)/shard_map/cond
  487.7 31.3 %copy-start.8 = (f32[128,64]{0,1:T(8,128)S(1)}, f32[128,64]{0,1:T(8,128)}, u32[]{:S(2)}) copy-start(f32[128,64]{0,1:T(8,128)} %get-tuple-element.35) | copy-start | bytes 98308 | tf_op jit(solution)/shard_map/cond
  493.5 25.5 %collective-permute-start = (bf16[128,64]{0,1:T(8,128)(2,1)S(1)}, bf16[128,64]{0,1:T(8,128)(2,1)S(1)}, u32[]{:S(2)}, u32[]{:S(2)}) collective-permute-start(bf16[128,64]{0,1:T(8,128)(2,1)S(1)} %get-tuple-element.134), channel_id=1, source_target_pairs={{8,0},{16,8},{24,16},{32,24},{40,32},{48,40},{56,48},{64,56},{72,6... | collective-permute-start | bytes 49160 | tf_op jit(solution)/shard_map/cond/branch_0_fun/ppermute | solution.py:33
  519.3 1.3 copy-start.9
  519.3 1.3 copy-start.13
Sparse Core Ops, SparseCore 0:
  111.0 42.0 all-gather.5
  155.6 93.6 all-gather.3

commit v3 on v2

--- a/solution.py
+++ b/solution.py
@@ -1,3 +1,5 @@
+import functools
+
 import jax
 import jax.numpy as jnp
 from jax import lax
@@ -12,31 +14,6 @@
 MESH_ID = pl.DeviceIdType.MESH
 
 
-def sent_together(arrays, axis, split_dim, concat_dim, along):
-    columns = [a.reshape(*a.shape[:along], -1) for a in arrays]
-    both = jnp.concatenate(columns, axis=along)
-    filled, at, outs = (
-        lax.all_to_all(both, axis, split_axis=split_dim, concat_axis=concat_dim, tiled=True),
-        0,
-        [],
-    )
-    for a, column in zip(arrays, columns):
-        slab = filled[..., at : at + column.shape[along]]
-        outs.append(slab.reshape(*slab.shape[:along], *a.shape[along:]))
-        at += column.shape[along]
-    return tuple(outs)
-
-
-def passed_along(value, axis, by):
-    peers = lax.axis_size(axis)
-    pairs = [(i, i + by) for i in range(peers) if 0 <= i + by < peers]
-    return lax.ppermute(value, axis, pairs)
-
-
-def picked(value, axis, root):
-    return lax.dynamic_index_in_dim(lax.all_gather(value, axis), root, 0, keepdims=False)
-
-
 def layer_norm(values):
     mean_row = jnp.mean(values, axis=-1, keepdims=True)
     centred = values - mean_row
@@ -44,135 +21,16 @@
     return centred * lax.rsqrt(variance + 1e-06)
 
 
-def rms_norm(values, gain_vec):
-    return values * lax.rsqrt(jnp.mean(values * values, axis=-1, keepdims=True) + 1e-06) * gain_vec
-
-
-def fold_keys(carried, queries, portion, scaling):
-    run_max, run_sum, run_out = carried
-    head_count = queries.shape[1]
-    head_size = queries.shape[2]
-    feature = head_count * head_size
-    key_rows = portion[:, :feature].reshape(portion.shape[0], head_count, head_size)
-    value_rows = portion[:, feature:].reshape(portion.shape[0], head_count, head_size)
-    scores = (
-        jnp.einsum("rhd,khd->rhk", queries, key_rows, preferred_element_type=jnp.float32) * scaling
-    )
-    new_max = jnp.maximum(run_max, jnp.max(scores, axis=-1))
-    weights = jnp.exp(scores - new_max[..., None])
-    run_sum = jnp.sum(weights, axis=-1)
-    run_out = jnp.einsum(
-        "rhk,khd->rhd", weights.astype(jnp.bfloat16), value_rows, preferred_element_type=jnp.float32
-    )
-    return (new_max, run_sum, run_out)
-
-
-def merge_states(maxima, totals, outputs):
-    top = jnp.max(maxima, axis=0)
-    factor = jnp.exp(maxima - top[None])
-    return (top, jnp.sum(totals * factor, axis=0), jnp.sum(outputs * factor[..., None], axis=0))
-
-
-def fresh_state(row_count, head_count, head_size):
-    return (
-        jnp.full((row_count, head_count), -1e30, jnp.float32),
-        jnp.zeros((row_count, head_count), jnp.float32),
-        jnp.zeros((row_count, head_count, head_size), jnp.float32),
-    )
-
-
-def key_value_rows(normed, qkv_weight, k_gain, feature):
-    projected = jnp.dot(normed, qkv_weight[:, feature:], preferred_element_type=jnp.float32)
-    key_part = rms_norm(projected[:, :feature], k_gain).astype(jnp.bfloat16)
-    return jnp.concatenate([key_part, projected[:, feature:].astype(jnp.bfloat16)], axis=1)
-
-
-def careful(
-    latents,
-    step_index,
-    tail_noise,
-    patch_weight,
-    time_table,
-    qkv_weight,
-    q_gain,
-    k_gain,
-    out_weight,
-    head_weight,
-):
-    feature = patch_weight.shape[1]
-    head_size = HEAD_DIM
-    head_count = feature // head_size
-    scaling = head_size ** (-0.5)
-    levels = time_table.shape[0]
-    frames = lax.axis_size("queue")
-    position = lax.axis_index("queue")
-    latent = latents[0]
-    tok_rows = latent.shape[0]
-    level_now = step_index[position]
-    level_before = jnp.where(position > 0, step_index[jnp.maximum(position - 1, 0)], -1)
-    one_hot = (jnp.arange(levels, dtype=jnp.int32) == level_now).astype(jnp.float32)[None, :]
-    modulation = jnp.dot(
-        one_hot, time_table.reshape(levels, 3 * feature), precision=lax.Precision.HIGHEST
-    ).reshape(3, feature)
-    hidden = jnp.dot(latent.astype(jnp.bfloat16), patch_weight, preferred_element_type=jnp.float32)
-    normed = (layer_norm(hidden) * (1.0 + modulation[1]) + modulation[0]).astype(jnp.bfloat16)
-    query_proj = jnp.dot(normed, qkv_weight[:, :feature], preferred_element_type=jnp.float32)
-    queries = rms_norm(query_proj, q_gain).astype(jnp.bfloat16)
-    key_value = key_value_rows(normed, qkv_weight, k_gain, feature)
-    whole_queries = lax.all_gather(queries, "tok", axis=0, tiled=True)
-    frame_rows = whole_queries.shape[0]
-    whole_queries = whole_queries.reshape(frame_rows, head_count, head_size)
-    state = fold_keys(
-        fresh_state(frame_rows, head_count, head_size),
-        whole_queries,
-        lax.all_gather(key_value, "queue", axis=0, tiled=True),
-        scaling,
-    )
-    parts = tuple(
-        (
-            part.astype(jnp.float32)
-            for part in sent_together(
-                (
-                    state[0][None].astype(jnp.bfloat16),
-                    state[1][None].astype(jnp.bfloat16),
-                    state[2][None].astype(jnp.bfloat16),
-                ),
-                "tok",
-                1,
-                0,
-                3,
-            )
-        )
-    )
-    carried = merge_states(parts[0], parts[1], parts[2])
-    run_max, run_sum, run_out = carried
-    attended = (run_out / run_sum[..., None]).reshape(tok_rows, feature).astype(jnp.bfloat16)
-    attn_out = jnp.dot(attended, out_weight, preferred_element_type=jnp.float32)
-    residual = hidden + modulation[2] * attn_out
-    velocity = jnp.dot(
-        residual.astype(jnp.bfloat16), head_weight, preferred_element_type=jnp.float32
-    )
-    sigma_now = (level_now.astype(jnp.float32) + 1.0) / levels
-    sigma_next = (level_before.astype(jnp.float32) + 1.0) / levels
-    updated = latent + (sigma_next - sigma_now) * velocity
-    arrived = passed_along(updated.astype(jnp.bfloat16), "queue", -1).astype(updated.dtype)
-    queue_next = jnp.where(position == frames - 1, tail_noise, arrived)
-    clean_frame = picked(updated.T.astype(jnp.bfloat16), "queue", 0).astype(jnp.float32)
-    channel_share = clean_frame.shape[0] // frames
-    leaving = lax.dynamic_slice_in_dim(clean_frame, position * channel_share, channel_share, 0)
-    return (velocity[None], queue_next[None], leaving)
-
-
 def dot_nt(a, b):
     return lax.dot_general(a, b, (((1,), (1,)), ((), ())), preferred_element_type=jnp.float32)
 
 
-def block_kernel(latent_in, mod_in, coef_in, patch_in, qkv_hbm, q_gain_in, k_gain_in, out_hbm,
-                 head_hbm, tail_hbm, vel_out, next_out, leaving_out, wide_out,
+def block_kernel(careful, latent_in, step_in, tail_hbm, patch_in, table_hbm, qkv_hbm, q_gain_in,
+                 k_gain_in, out_hbm, head_hbm, vel_out, next_out, leaving_out, wide_out,
                  q_in, kv_in, q_all, kv_all, o_send, o_recv, a_send, out,
-                 w_buf, ow_buf, hw_buf, tail_buf, hidden_buf, normed_buf, proj_buf,
+                 w_buf, ow_buf, hw_buf, tail_buf, table_buf, hidden_buf, normed_buf, proj_buf,
                  size_buf, u_send, u_recv, lv_send, lv_recv,
-                 w_sem, ow_sem, hw_sem, tail_sem, f_s, f_r, u_s, u_r, lv_s, lv_r,
+                 w_sem, ow_sem, hw_sem, tail_sem, table_sem, f_s, f_r, u_s, u_r, lv_s, lv_r,
                  xq_s, xq_r, xk_s, xk_r, yq_s, yq_r, zk_s, zk_r, ck_s, ck_r,
                  oy_s, oy_r, ox_s, ox_r):
     queue = lax.axis_index("queue")
@@ -295,7 +153,10 @@
     out_copy = pltpu.make_async_copy(out_hbm, ow_buf, ow_sem)
     head_copy = pltpu.make_async_copy(head_hbm, hw_buf, hw_sem)
     tail_copy = pltpu.make_async_copy(tail_hbm, tail_buf, tail_sem)
-    for b in (3, 4, 5, 6, 7, 8, 0, 1, 2):
+    table_copy = pltpu.make_async_copy(table_hbm, table_buf, table_sem)
+    weight(3).start()
+    table_copy.start()
+    for b in (4, 5, 6, 7, 8, 0, 1, 2):
         weight(b).start()
     barrier = pltpu.get_barrier_semaphore()
     for n in range(1, 16):
@@ -308,11 +169,15 @@
         pl.semaphore_signal(barrier, inc=1, device_id=device(x, hop(y, d), z, core),
                             device_id_type=MESH_ID)
 
-    hidden = jnp.dot(latent_in[...].astype(jnp.bfloat16), patch_in[...],
-                     preferred_element_type=jnp.float32)
+    level_now = step_in[queue]
+    level_before = jnp.where(queue > 0, step_in[jnp.maximum(queue - 1, 0)], -1)
+    step = (level_before - level_now).astype(jnp.float32) * (1.0 / 64)
+    hidden = lax.dot_general(latent_in[...].astype(jnp.bfloat16), patch_in[...],
+                             (((0,), (0,)), ((), ())), preferred_element_type=jnp.float32)
     hidden_buf[...] = hidden
-    normed_buf[...] = (layer_norm(hidden) * (1.0 + mod_in[1:2, :]) + mod_in[0:1, :]).astype(
-        jnp.bfloat16)
+    table_copy.wait()
+    shift, scale, gate = [table_buf[n, pl.ds(level_now, 1), :] for n in range(3)]
+    normed_buf[...] = (layer_norm(hidden) * (1.0 + scale) + shift).astype(jnp.bfloat16)
 
     def project(b, at):
         weight(b).wait()
@@ -333,7 +198,7 @@
 
     square = project(3, 0) + project(4, 1) + project(5, 2)
     factor = lax.rsqrt(square * (1.0 / 1536) + 1e-06)
-    keys = (proj_buf[...] * factor * k_gain_in[...]).astype(jnp.bfloat16)
+    keys = (proj_buf[...] * factor * k_gain_in[...].reshape(1, 1536)).astype(jnp.bfloat16)
     for n in range(12):
         kv_in[n, 0] = keys[:, n * 128:(n + 1) * 128]
     key_size = top_norm(keys)
@@ -360,7 +225,7 @@
     head_copy.start()
     tail_copy.start()
     factor = lax.rsqrt(square * (1.0 / 1536) + 1e-06) * (HEAD_DIM ** (-0.5) * LOG2E)
-    queries = (proj_buf[...] * factor * q_gain_in[...]).astype(jnp.bfloat16)
+    queries = (proj_buf[...] * factor * q_gain_in[...].reshape(1, 1536)).astype(jnp.bfloat16)
     for n in range(12):
         q_in[n] = queries[:, n * 128:(n + 1) * 128]
     for h in range(3):
@@ -397,17 +262,24 @@
         for d in (1, 2, 3):
             y_part_in(h, d).wait_recv()
         parts = [o_send.at[h, y]] + [o_recv.at[h, hop(y, d)] for d in (1, 2, 3)]
-        den = jnp.zeros((4, 128), jnp.float32)
-        for part in parts:
-            tail = part[512:528, :].astype(jnp.float32)
-            den = den + (tail[0:4] + tail[4:8])
-        inv = (1.0 / VALUE_SHRINK) / den
+        tails = [part[512:528, :].astype(jnp.float32) for part in parts]
+        dens = [tail[0:4] + tail[4:8] for tail in tails]
+        if careful:
+            tops = [tail[8:12] + tail[12:16] for tail in tails]
+            top = functools.reduce(jnp.maximum, tops)
+            factors = [jnp.exp2(own - top) for own in tops]
+            dens = [den * factor for den, factor in zip(dens, factors)]
+        inv = (1.0 / VALUE_SHRINK) / (dens[0] + dens[1] + dens[2] + dens[3])
+
+        def column(values, g):
+            return jnp.transpose(jnp.broadcast_to(values[g:g + 1, :], (128, 128)))
+
         for g in range(4):
-            num = parts[0][g * 128:(g + 1) * 128, :].astype(jnp.float32)
-            for part in parts[1:]:
-                num = num + part[g * 128:(g + 1) * 128, :].astype(jnp.float32)
-            column = jnp.transpose(jnp.broadcast_to(inv[g:g + 1, :], (128, 128)))
-            a_send[h, g] = (num * column).astype(jnp.bfloat16)
+            nums = [part[g * 128:(g + 1) * 128, :].astype(jnp.float32) for part in parts]
+            if careful:
+                nums = [num * column(factor, g) for num, factor in zip(nums, factors)]
+            num = (nums[0] + nums[1]) + (nums[2] + nums[3])
+            a_send[h, g] = (num * column(inv, g)).astype(jnp.bfloat16)
         out[x * 3 + h] = a_send[h, x]
         for d in (1, 3, 2):
             x_back(h, d).start()
@@ -422,18 +294,32 @@
 
         queries = q_all[h, to]
         scores = dot_nt(queries, kv_all[h, 0])
+
+        def lanes(values, op):
+            return functools.reduce(op, [values[:, n * 128:(n + 1) * 128] for n in range(32)])
+
+        def as_rows(values, op):
+            return jnp.concatenate(
+                [op(jnp.transpose(values[g * 128:(g + 1) * 128, :]), axis=0, keepdims=True)
+                 for g in range(4)], axis=0)
+
+        if careful:
+            most = lanes(scores, jnp.maximum)
+            scores = scores - jnp.ceil(jnp.max(most, axis=1, keepdims=True))
+            top = jnp.ceil(as_rows(most, jnp.max))
+        else:
+            top = jnp.zeros((4, 128), jnp.float32)
         weights = jnp.exp2(scores)
-        total = weights[:, 0:128]
-        for n in range(1, 32):
-            total = total + weights[:, n * 128:(n + 1) * 128]
+        den = as_rows(lanes(weights, jnp.add), jnp.sum)
         num = jnp.dot(weights.astype(jnp.bfloat16), kv_all[h, 1],
                       preferred_element_type=jnp.float32)
         o_send[h, to, 0:512, :] = num.astype(jnp.bfloat16)
-        rows_of = [jnp.sum(jnp.transpose(total[g * 128:(g + 1) * 128, :]), axis=0, keepdims=True)
-                   for g in range(4)]
-        den = jnp.concatenate(rows_of, axis=0)
-        high = den.astype(jnp.bfloat16).astype(jnp.float32)
-        tail = jnp.concatenate([high, den - high, jnp.zeros((8, 128), jnp.float32)], axis=0)
+
+        def two(values):
+            high = values.astype(jnp.bfloat16).astype(jnp.float32)
+            return [high, values - high]
+
+        tail = jnp.concatenate(two(den) + two(top), axis=0)
         o_send[h, to, 512:528, :] = tail.astype(jnp.bfloat16)
 
         @pl.when(i < 3)
@@ -469,8 +355,7 @@
     lax.fori_loop(0, 12, chunk, 0)
     sizes = size_take(3)
     wide = jnp.maximum(sizes[0:1] * sizes[1:2] - SAFE_LOG2 * SAFE_LOG2, sizes[2:3] - 2.0)
-    wide = jnp.max(wide, axis=1, keepdims=True)
-    wide_out[...] = jnp.broadcast_to(wide, (8, 128))
+    wide_out[0] = jnp.where(jnp.max(wide) > 0.0, 1, 0)
     combine(2)
     out_copy.wait()
     head_copy.wait()
@@ -480,11 +365,10 @@
             x_back_in(h, d).wait_recv()
     attended = jnp.concatenate([out[n] for n in range(12)], axis=1)
     attn_out = jnp.dot(attended, ow_buf[...], preferred_element_type=jnp.float32)
-    residual = hidden_buf[...] + mod_in[2:3, :] * attn_out
-    velocity = jnp.dot(residual.astype(jnp.bfloat16), hw_buf[...],
-                       preferred_element_type=jnp.float32)
+    residual = hidden_buf[...] + table_buf[2, pl.ds(level_now, 1), :] * attn_out
+    velocity = dot_nt(hw_buf[...], residual.astype(jnp.bfloat16))
     vel_out[...] = velocity
-    updated = jnp.transpose(latent_in[...] + coef_in[0] * velocity)
+    updated = latent_in[...] + step * velocity
     u_send[...] = updated
 
     send_next = remote(u_send, u_recv, u_s, u_r, (lax.rem(queue + 15, 16), tok))
@@ -512,7 +396,7 @@
     @pl.when(queue < 15)
     def _():
         take_next.wait_recv()
-        next_out[...] = jnp.transpose(u_recv[...])
+        next_out[...] = u_recv[...]
 
     @pl.when(queue > 0)
     def _():
@@ -540,21 +424,21 @@
             c_keys(h, d).wait_send()
 
 
-def block(*operands):
+def block(careful, *operands):
     sems = [pltpu.SemaphoreType.DMA((3, 4))] * 14
     vmem, hbm = pl.BlockSpec(memory_space=pltpu.VMEM), pl.BlockSpec(memory_space=pltpu.HBM)
     smem = pl.BlockSpec(memory_space=pltpu.SMEM)
     f32, bf16, dma = jnp.float32, jnp.bfloat16, pltpu.SemaphoreType.DMA
     return pl.pallas_call(
-        block_kernel,
+        functools.partial(block_kernel, careful),
         out_shape=[
-            jax.ShapeDtypeStruct((128, 64), f32),
-            jax.ShapeDtypeStruct((128, 64), f32),
+            jax.ShapeDtypeStruct((64, 128), f32),
+            jax.ShapeDtypeStruct((64, 128), f32),
             jax.ShapeDtypeStruct((4, 128), f32),
-            jax.ShapeDtypeStruct((8, 128), f32),
+            jax.ShapeDtypeStruct((1,), jnp.int32),
         ],
-        in_specs=[vmem, vmem, smem, vmem, hbm, vmem, vmem, hbm, hbm, hbm],
-        out_specs=[vmem] * 4,
+        in_specs=[vmem, smem, hbm, vmem, hbm, hbm, vmem, vmem, hbm, hbm],
+        out_specs=[vmem, vmem, vmem, smem],
         scratch_shapes=[
             pltpu.VMEM((12, 128, 128), bf16),
             pltpu.VMEM((12, 2, 128, 128), bf16),
@@ -566,8 +450,9 @@
             pltpu.VMEM((12, 128, 128), bf16),
             pltpu.VMEM((9, 1536, 512), bf16),
             pltpu.VMEM((1536, 1536), bf16),
-            pltpu.VMEM((1536, 64), bf16),
-            pltpu.VMEM((128, 64), f32),
+            pltpu.VMEM((64, 1536), bf16),
+            pltpu.VMEM((64, 128), f32),
+            pltpu.VMEM((3, 64, 1536), f32),
             pltpu.VMEM((128, 1536), f32),
             pltpu.VMEM((128, 1536), bf16),
             pltpu.VMEM((128, 1536), f32),
@@ -576,11 +461,11 @@
             pltpu.VMEM((64, 128), f32),
             pltpu.VMEM((16, 8, 128), f32),
             pltpu.VMEM((8, 128), f32),
-            dma((9,)), dma(()), dma(()), dma(()), dma((4, 4)), dma((4, 4)),
+            dma((9,)), dma(()), dma(()), dma(()), dma(()), dma((4, 4)), dma((4, 4)),
             dma(()), dma(()), dma((16,)), dma(()),
         ] + sems,
         compiler_params=pltpu.CompilerParams(
-            collective_id=1, has_side_effects=True, vmem_limit_bytes=58 * 2**20),
+            collective_id=2 if careful else 1, has_side_effects=True, vmem_limit_bytes=58 * 2**20),
         cost_estimate=pl.CostEstimate(flops=16 * 10**9, bytes_accessed=40 * 10**6,
                                       transcendentals=25 * 10**6),
     )(*operands)
@@ -598,20 +483,13 @@
     out_weight,
     head_weight,
 ):
-    levels = time_table.shape[0]
-    position = lax.axis_index("queue")
-    level_now = step_index[position]
-    level_before = jnp.where(position > 0, step_index[jnp.maximum(position - 1, 0)], -1)
-    modulation = lax.dynamic_index_in_dim(time_table, level_now, 0, keepdims=False)
-    sigma_now = (level_now.astype(jnp.float32) + 1.0) / levels
-    sigma_next = (level_before.astype(jnp.float32) + 1.0) / levels
-    velocity, queue_next, leaving, wide = block(
-        latents[0], modulation, (sigma_next - sigma_now)[None], patch_weight, qkv_weight,
-        q_gain[None], k_gain[None], out_weight, head_weight, tail_noise)
-    args = (latents, step_index, tail_noise, patch_weight, time_table, qkv_weight, q_gain,
-            k_gain, out_weight, head_weight)
-    return lax.cond(wide[0, 0] <= 0.0, lambda *_: (velocity[None], queue_next[None], leaving),
-                    careful, *args)
+    operands = (latents[0].T, step_index, tail_noise.T, patch_weight,
+                time_table.transpose(1, 0, 2), qkv_weight, q_gain, k_gain, out_weight,
+                head_weight.T)
+    *fast, wide = block(False, *operands)
+    velocity, queue_next, leaving = lax.cond(
+        wide[0] == 0, lambda *_: tuple(fast), lambda *a: tuple(block(True, *a)[:3]), *operands)
+    return velocity.T[None], queue_next.T[None], leaving
 
 
 def solution(mesh):

time: 538 us -> 198 us (0.37); the launches traced: 528 us -> 198 us
  waiting for transfers between devices: 157 us -> 0 us
  Pallas kernels: 81 us -> 194 us
  local copies, waits for them, and re-layouts: 113 us -> 1.84 us
  matrix products: 85.5 us -> 0 us
  other arithmetic: 43 us -> 0 us
  blocking collectives: 22.2 us -> 0 us
  between operations: 18.5 us -> 1.38 us
  starting transfers between devices: 6.79 us -> 0 us
    all_gather x2 -> x0, waiting for transfers between devices: 120 us -> none  [the longest x1 84.2 us: careful(): lax.all_gather(key_value, 'queue', axis=0, tiled=True)]
    pallas_call x1 -> x2, Pallas kernels: 81 us -> 194 us  [block(): pl.pallas_call(functools.partial(block_kernel, careful), out_shape=[jax.S...]
    dot_general x7 -> x0, matrix products: 85.5 us -> none  [the longest x1 37 us: fold_keys(): jnp.einsum('rhd,khd->rhk', queries, key_rows, preferred_element_type=jnp....]
    cond x18 -> x0, local copies, waits for them, and re-layouts: 39.9 us -> none
    all_to_all x1 -> x0, waiting for transfers between devices: 36.8 us -> none  [sent_together(): lax.all_to_all(both, axis, split_axis=split_dim, concat_axis=concat_dim,...]
    slice x6 -> x0, local copies, waits for them, and re-layouts: 35.7 us -> none  [the longest x2 18.9 us: fold_keys(): portion[:, :feature].reshape(portion.shape[0], head_count, head_size)]
    reduce_sum x5 -> x0, other arithmetic: 33.4 us -> none  [the longest x1 31 us: fold_keys(): run_sum = jnp.sum(weights, axis=-1)]
    all_gather x1 -> x0, blocking collectives: 22.2 us -> none  [picked(): lax.all_gather(value, axis)]
  transfers between devices with their start and end apart: 4 -> 0, of which waited for: 3 -> 0; matrix products, arithmetic and copies ran while one was open for 4% -> 0% of each run, Pallas kernels for 0% -> 0%
where the time goes in v3:
time: 198 us
  Pallas kernels  194 us (98%)
    pallas_call x2, Pallas kernels, block(): pl.pallas_call(functools.partial(block_kernel, careful), out_shape=[jax.S...  194 us

profile of v3, /device:TPU:1, one launch (start us, length us, event | category | flops | bytes accessed | tf_op | source)
XLA Modules:
  0.0 197.9 jit_solution(7102790746842911831)
XLA Ops:
  0.6 0.0 copy-start
  0.6 0.0 copy-start.1
  0.7 0.0 copy-start.2
  0.7 0.0 copy-start.3
  0.7 0.0 copy-start.4
  0.7 0.0 copy-start.5
  0.7 0.0 copy-start.6
  0.7 85.0 %shard_map.121 = (f32[64,128]{1,0:T(8,128)S(1)}, f32[64,128]{1,0:T(8,128)S(1)}, f32[4,128]{1,0:T(4,128)S(1)}, s32[1]{0:T(128)}) custom-call(f32[64,128]{1,0:T(8,128)} %bitcast.19, s32[16]{0:T(128)} %step_in.1, f32[64,128]{1,0:T(8,128)} %bitcast.21, bf16[64,1536]{1,0:T(8,128)(2,1)} %patch_in.1, f32[3,64,1536]{2,1,0:T(8,128)} %bitcast.15, ...), custom_call_target="tpu_custom_call" | custom-call | flops 16000000000 | bytes 40000000 | tf_op jit(solution)/shard_map/pallas_call | solution.py:432
  86.3 0.0 copy-done
  86.3 0.0 copy-done.1
  86.3 0.0 copy-done.2
  86.4 0.0 copy-done.3
  86.4 0.0 copy-done.4
  86.4 0.0 copy-done.5
  86.4 0.0 copy-done.6
  86.4 109.7 %conditional.1 = ((f32[64,128]{1,0:T(8,128)S(1)}, f32[64,128]{1,0:T(8,128)S(1)}, f32[4,128]{1,0:T(4,128)S(1)})) conditional(s32[]{:T(128)} %bitcast.5, (f32[64,128]{1,0:T(8,128)S(1)}, s32[16]{0:T(128)S(1)}, f32[64,128]{1,0:T(8,128)}, bf16[64,1536]{1,0:T(8,128)(2,1)S(1)}, f32[3,64,1536]{2,1,0:T(8,128)S(1)}, /*index=5*/bf16[1536,4608]{1,0:T(8,128)(2,1)}, ...), branch_computations={%region_0.0_spmd, %region_1.0_spmd} | conditional | flops 16000000000 | bytes 40000032 | solution.py:490
  86.6 109.2 %branch_0_fun.1 = (f32[64,128]{1,0:T(8,128)S(1)}, f32[64,128]{1,0:T(8,128)S(1)}, f32[4,128]{1,0:T(4,128)S(1)}, s32[1]{0:T(128)}) custom-call(f32[64,128]{1,0:T(8,128)S(1)} %get-tuple-element.26.latent_in, s32[16]{0:T(128)S(1)} %get-tuple-element.27.step_in, f32[64,128]{1,0:T(8,128)} %get-tuple-element.28.tail_hbm, ...), custom_call_target="tpu_custom_call" | custom-call | flops 16000000000 | bytes 40000000 | tf_op jit(solution)/shard_map/cond/branch_0_fun/pallas_call | solution.py:432
  196.1 0.6 copy.22
  196.7 0.6 copy.23
  197.3 0.6 copy.24
Async XLA Ops:
  0.6 85.7 %copy-start = (bf16[1536,1536]{1,0:T(8,128)(2,1)S(1)}, bf16[1536,1536]{1,0:T(8,128)(2,1)}, u32[]{:S(2)}) copy-start(bf16[1536,1536]{1,0:T(8,128)(2,1)} %out_hbm.1) | copy-start | bytes 14155780
  0.6 85.7 %copy-start.1 = (f32[64,3,1536]{2,0,1:T(8,128)S(1)}, f32[64,3,1536]{2,0,1:T(8,128)}, u32[]{:S(2)}) copy-start(f32[64,3,1536]{2,0,1:T(8,128)} %param.16) | copy-start | bytes 3538948
  0.7 85.7 %copy-start.2 = (bf16[64,1536]{1,0:T(8,128)(2,1)S(1)}, bf16[64,1536]{1,0:T(8,128)(2,1)}, u32[]{:S(2)}) copy-start(bf16[64,1536]{1,0:T(8,128)(2,1)} %patch_in.1) | copy-start | bytes 589828
  0.7 85.7 %copy-start.3 = (f32[1,128,64]{1,2,0:T(8,128)S(1)}, f32[1,128,64]{1,2,0:T(8,128)}, u32[]{:S(2)}) copy-start(f32[1,128,64]{1,2,0:T(8,128)} %param.12) | copy-start | bytes 98308
  0.7 85.7 %copy-start.4 = (f32[1536]{0:T(1024)S(1)}, f32[1536]{0:T(1024)}, u32[]{:S(2)}) copy-start(f32[1536]{0:T(1024)} %q_gain_in.1) | copy-start | bytes 18436
  0.7 85.7 %copy-start.5 = (f32[1536]{0:T(1024)S(1)}, f32[1536]{0:T(1024)}, u32[]{:S(2)}) copy-start(f32[1536]{0:T(1024)} %k_gain_in.1) | copy-start | bytes 18436
  0.7 85.7 %copy-start.6 = (s32[16]{0:T(128)S(1)}, s32[16]{0:T(128)}, u32[]{:S(2)}) copy-start(s32[16]{0:T(128)} %step_in.1) | copy-start | bytes 196

commit v4 on v3

--- a/solution.py
+++ b/solution.py
@@ -28,7 +28,7 @@
 def block_kernel(careful, latent_in, step_in, tail_hbm, patch_in, table_hbm, qkv_hbm, q_gain_in,
                  k_gain_in, out_hbm, head_hbm, vel_out, next_out, leaving_out, wide_out,
                  q_in, kv_in, q_all, kv_all, o_send, o_recv, a_send, out,
-                 w_buf, ow_buf, hw_buf, tail_buf, table_buf, hidden_buf, normed_buf, proj_buf,
+                 w_buf, ow_buf, hw_buf, tail_buf, table_buf, hidden_buf, normed_buf, proj_buf, num_buf, den_buf,
                  size_buf, u_send, u_recv, lv_send, lv_recv,
                  w_sem, ow_sem, hw_sem, tail_sem, table_sem, f_s, f_r, u_s, u_r, lv_s, lv_r,
                  xq_s, xq_r, xk_s, xk_r, yq_s, yq_r, zk_s, zk_r, ck_s, ck_r,
@@ -46,79 +46,78 @@
     def hop(v, d):
         return lax.rem(v + d + 4, 4)
 
-    slot = z * 2 + core
-
     def rows(n, size):
         return pl.ds(pl.multiple_of(n * size, size), size)
+
+    def coordinate(axis):
+        if isinstance(axis, int):
+            return (x, y, z)[axis]
+        return jnp.where(axis == 0, x, jnp.where(axis == 1, y, z))
+
+    def turned(h, by):
+        return (h + by) % 3 if isinstance(h, int) else lax.rem(h + by, 3)
+
+    def peer(axis, d):
+        at = hop(coordinate(axis), d)
+        if isinstance(axis, int):
+            return device(*[at if axis == n else v for n, v in enumerate((x, y, z))], core)
+        return device(*[jnp.where(axis == n, at, v) for n, v in enumerate((x, y, z))], core)
+
+    place = {0: 0, 1: 1, 3: 2, 2: 3}
 
     def remote(src, dst, s, r, dev):
         return pltpu.make_async_remote_copy(src_ref=src, dst_ref=dst, send_sem=s, recv_sem=r,
                                             device_id=dev, device_id_type=MESH_ID)
 
     def x_query(h, d):
-        g = hop(x, d)
-        return remote(q_in.at[g * 3 + h], q_all.at[h, y, rows(x, 128)],
-                      xq_s.at[h, d], xq_r.at[h, d], device(g, y, z, core))
+        mine = coordinate(h)
+        return remote(q_in.at[hop(mine, d) * 3 + h], q_all.at[h, 0, rows(mine, 128)],
+                      xq_s.at[h, d], xq_r.at[h, d], peer(h, d))
 
     def x_query_in(h, d):
-        g = hop(x, -d)
-        return remote(q_in.at[x * 3 + h], q_all.at[h, y, rows(g, 128)],
-                      xq_s.at[h, d], xq_r.at[h, d], device(g, y, z, core))
+        mine = coordinate(h)
+        return remote(q_in.at[mine * 3 + h], q_all.at[h, 0, rows(hop(mine, -d), 128)],
+                      xq_s.at[h, d], xq_r.at[h, d], peer(h, -d))
 
     def x_keys(h, d):
-        g = hop(x, d)
-        return remote(kv_in.at[g * 3 + h], kv_all.at[h, :, rows(slot * 4 + x, 128)],
-                      xk_s.at[h, d], xk_r.at[h, d], device(g, y, z, core))
+        mine = coordinate(h)
+        return remote(kv_in.at[hop(mine, d) * 3 + h], kv_all.at[h, :, rows(core * 4 + mine, 128)],
+                      xk_s.at[h, d], xk_r.at[h, d], peer(h, d))
 
     def x_keys_in(h, d):
-        g = hop(x, -d)
-        return remote(kv_in.at[x * 3 + h], kv_all.at[h, :, rows(slot * 4 + g, 128)],
-                      xk_s.at[h, d], xk_r.at[h, d], device(g, y, z, core))
-
-    def y_query(h, d):
-        return remote(q_all.at[h, y], q_all.at[h, y], yq_s.at[h, d], yq_r.at[h, d],
-                      device(x, hop(y, d), z, core))
-
-    def y_query_in(h, d):
-        g = hop(y, -d)
-        return remote(q_all.at[h, g], q_all.at[h, g], yq_s.at[h, d], yq_r.at[h, d],
-                      device(x, g, z, core))
-
-    def z_keys(h, d):
-        at = kv_all.at[h, :, rows(slot, 512)]
-        return remote(at, at, zk_s.at[h, d], zk_r.at[h, d], device(x, y, hop(z, d), core))
-
-    def z_keys_in(h, d):
-        g = hop(z, -d)
-        at = kv_all.at[h, :, rows(g * 2 + core, 512)]
-        return remote(at, at, zk_s.at[h, d], zk_r.at[h, d], device(x, y, g, core))
-
-    def c_keys(h, d):
-        at = kv_all.at[h, :, rows(hop(z, -d) * 2 + core, 512)]
+        mine = coordinate(h)
+        return remote(kv_in.at[mine * 3 + h],
+                      kv_all.at[h, :, rows(core * 4 + hop(mine, -d), 128)],
+                      xk_s.at[h, d], xk_r.at[h, d], peer(h, -d))
+
+    def y_query(h, d, arriving=False):
+        return remote(q_all.at[h, 0], q_all.at[h, 4 - d], yq_s.at[h, d], yq_r.at[h, d],
+                      peer(turned(h, 1), -d if arriving else d))
+
+    def key_place(h, d, half):
+        return kv_all.at[h, :, rows(place[(4 - d) % 4] * 2 + half, 512)]
+
+    def z_keys(h, d, arriving=False):
+        return remote(key_place(h, 0, core), key_place(h, d, core), zk_s.at[h, d],
+                      zk_r.at[h, d], peer(turned(h, 2), -d if arriving else d))
+
+    def c_keys(h, d, arriving=False):
+        at = key_place(h, d, 1 - core if arriving else core)
         return remote(at, at, ck_s.at[h, d], ck_r.at[h, d], device(x, y, z, 1 - core))
 
-    def c_keys_in(h, d):
-        at = kv_all.at[h, :, rows(hop(z, -d) * 2 + 1 - core, 512)]
-        return remote(at, at, ck_s.at[h, d], ck_r.at[h, d], device(x, y, z, 1 - core))
-
-    def y_part(h, d):
-        return remote(o_send.at[h, hop(y, d)], o_recv.at[h, y], oy_s.at[h, d], oy_r.at[h, d],
-                      device(x, hop(y, d), z, core))
-
-    def y_part_in(h, d):
-        g = hop(y, -d)
-        return remote(o_send.at[h, g], o_recv.at[h, g], oy_s.at[h, d], oy_r.at[h, d],
-                      device(x, g, z, core))
+    def y_part(h, d, arriving=False):
+        return remote(o_send.at[h, d], o_recv.at[h, 4 - d], oy_s.at[h, d], oy_r.at[h, d],
+                      peer(turned(h, 1), -d if arriving else d))
 
     def x_back(h, d):
-        g = hop(x, d)
-        return remote(a_send.at[h, g], out.at[x * 3 + h], ox_s.at[h, d], ox_r.at[h, d],
-                      device(g, y, z, core))
+        mine = coordinate(h)
+        return remote(a_send.at[h, hop(mine, d)], out.at[mine * 3 + h],
+                      ox_s.at[h, d], ox_r.at[h, d], peer(h, d))
 
     def x_back_in(h, d):
-        g = hop(x, -d)
-        return remote(a_send.at[h, g], out.at[g * 3 + h], ox_s.at[h, d], ox_r.at[h, d],
-                      device(g, y, z, core))
+        mine = coordinate(h)
+        return remote(a_send.at[h, hop(mine, -d)], out.at[hop(mine, -d) * 3 + h],
+                      ox_s.at[h, d], ox_r.at[h, d], peer(h, -d))
 
     def size_step(stage, d, arriving=False):
         if stage == 0:
@@ -217,8 +216,10 @@
     for h in range(3):
         for d in (1, 3, 2):
             x_keys(h, d).start()
+    for h in range(3):
+        mine = coordinate(h)
         for kv in range(2):
-            kv_all[h, kv, rows(slot * 4 + x, 128), :] = kv_in[x * 3 + h, kv]
+            kv_all[h, kv, rows(core * 4 + mine, 128), :] = kv_in[mine * 3 + h, kv]
 
     square = project(0, 0) + project(1, 1) + project(2, 2)
     out_copy.start()
@@ -231,37 +232,48 @@
     for h in range(3):
         for d in (1, 3, 2):
             x_query(h, d).start()
-        q_all[h, y, rows(x, 128), :] = q_in[x * 3 + h]
+        q_all[h, 0, rows(coordinate(h), 128), :] = q_in[coordinate(h) * 3 + h]
     size_buf[0, 0] = jnp.concatenate(
         [top_norm(queries), key_size, value_size, jnp.zeros((5, 128), jnp.float32)], axis=0)
     size_send(0)
 
-    def spread(h):
+    def spread_keys(h):
         for d in (1, 3, 2):
             x_keys_in(h, d).wait_recv()
-        for d in (1, 3, 2):
+        for d in (1, 3):
             z_keys(h, d).start()
         c_keys(h, 0).start()
+        z_keys(h, 2).start()
+
+    def spread_queries(h):
         for d in (1, 3, 2):
             x_query_in(h, d).wait_recv()
         for d in (1, 3, 2):
             y_query(h, d).start()
 
-    def share(h, d):
-        z_keys_in(h, d).wait_recv()
-        c_keys(h, d).start()
-
-    for h in range(3):
-        spread(h)
-    for d in (1, 3, 2):
-        share(0, d)
-    for d in (0, 1, 3, 2):
-        c_keys_in(0, d).wait_recv()
+    def share(h, *steps):
+        for d in steps:
+            z_keys(h, d, True).wait_recv()
+            c_keys(h, d).start()
+
+    def shared(h, *steps):
+        for d in steps:
+            c_keys(h, d, True).wait_recv()
+
+    spread_keys(0)
+    spread_keys(1)
+    spread_queries(0)
+    spread_keys(2)
+    spread_queries(1)
+    spread_queries(2)
+    share(0, 1, 3)
+    shared(0, 0, 1, 3)
 
     def combine(h):
         for d in (1, 2, 3):
-            y_part_in(h, d).wait_recv()
-        parts = [o_send.at[h, y]] + [o_recv.at[h, hop(y, d)] for d in (1, 2, 3)]
+            y_part(h, d, True).wait_recv()
+        parts = [o_send.at[h, 0]] + [o_recv.at[h, d] for d in (1, 2, 3)]
+        mine = coordinate(h)
         tails = [part[512:528, :].astype(jnp.float32) for part in parts]
         dens = [tail[0:4] + tail[4:8] for tail in tails]
         if careful:
@@ -280,65 +292,103 @@
                 nums = [num * column(factor, g) for num, factor in zip(nums, factors)]
             num = (nums[0] + nums[1]) + (nums[2] + nums[3])
             a_send[h, g] = (num * column(inv, g)).astype(jnp.bfloat16)
-        out[x * 3 + h] = a_send[h, x]
+        out[mine * 3 + h] = a_send[h, mine]
         for d in (1, 3, 2):
             x_back(h, d).start()
 
-    def chunk(t, carry):
-        h, i = t // 4, lax.rem(t, 4)
-        to = lax.rem(y + i + 1, 4)
-
-        @pl.when(i < 3)
-        def _():
-            y_query_in(h, 3 - i).wait_recv()
-
-        queries = q_all[h, to]
-        scores = dot_nt(queries, kv_all[h, 0])
-
-        def lanes(values, op):
-            return functools.reduce(op, [values[:, n * 128:(n + 1) * 128] for n in range(32)])
-
-        def as_rows(values, op):
-            return jnp.concatenate(
-                [op(jnp.transpose(values[g * 128:(g + 1) * 128, :]), axis=0, keepdims=True)
-                 for g in range(4)], axis=0)
-
+    def lanes(values, op):
+        return functools.reduce(op, [values[:, n:n + 128] for n in range(0, values.shape[1], 128)])
+
+    def as_rows(values, op):
+        return jnp.concatenate(
+            [op(jnp.transpose(values[g * 128:(g + 1) * 128, :]), axis=0, keepdims=True)
+             for g in range(4)], axis=0)
+
+    def two(values):
+        high = values.astype(jnp.bfloat16).astype(jnp.float32)
+        return [high, values - high]
+
+    def fold(h, at, first, last):
+        scores = dot_nt(q_all[h, at], kv_all[h, 0, first:last, :])
+        top = jnp.zeros((4, 128), jnp.float32)
         if careful:
             most = lanes(scores, jnp.maximum)
             scores = scores - jnp.ceil(jnp.max(most, axis=1, keepdims=True))
             top = jnp.ceil(as_rows(most, jnp.max))
+        weights = jnp.exp2(scores)
+        num = jnp.dot(weights.astype(jnp.bfloat16), kv_all[h, 1, first:last, :],
+                      preferred_element_type=jnp.float32)
+        return num, lanes(weights, jnp.add), top
+
+    def write_part(h, at, num, den, top):
+        o_send[h, at, 0:512, :] = num.astype(jnp.bfloat16)
+        tail = jnp.concatenate(two(as_rows(den, jnp.sum)) + two(top), axis=0)
+        o_send[h, at, 512:528, :] = tail.astype(jnp.bfloat16)
+
+    def early(at, carry):
+        for d in (1, 2, 3):
+            @pl.when(at == 4 - d)
+            def _():
+                y_query(0, d, True).wait_recv()
+
+        if not careful:
+            num, den, _ = fold(0, at, 0, 3072)
+            num_buf[at] = num
+            den_buf[at] = den
+
+        @pl.when(at == 1)
+        def _():
+            share(0, 2)
+
+        @pl.when(at == 2)
+        def _():
+            share(1, 1, 3)
+
+        @pl.when(at == 3)
+        def _():
+            share(1, 2)
+
+        return carry
+
+    lax.fori_loop(0, 4, early, 0)
+    shared(0, 2)
+
+    def chunk(t, carry):
+        h, i = t // 4, lax.rem(t, 4)
+        at = lax.rem(i + 1, 4)
+
+        @pl.when(jnp.logical_and(h > 0, i < 3))
+        def _():
+            y_query(h, 3 - i, True).wait_recv()
+
+        if careful:
+            write_part(h, at, *fold(h, at, 0, 4096))
         else:
-            top = jnp.zeros((4, 128), jnp.float32)
-        weights = jnp.exp2(scores)
-        den = as_rows(lanes(weights, jnp.add), jnp.sum)
-        num = jnp.dot(weights.astype(jnp.bfloat16), kv_all[h, 1],
-                      preferred_element_type=jnp.float32)
-        o_send[h, to, 0:512, :] = num.astype(jnp.bfloat16)
-
-        def two(values):
-            high = values.astype(jnp.bfloat16).astype(jnp.float32)
-            return [high, values - high]
-
-        tail = jnp.concatenate(two(den) + two(top), axis=0)
-        o_send[h, to, 512:528, :] = tail.astype(jnp.bfloat16)
+            @pl.when(h == 0)
+            def _():
+                num, den, top = fold(0, at, 3072, 4096)
+                write_part(0, at, num_buf[at] + num, den_buf[at] + den, top)
+
+            @pl.when(h > 0)
+            def _():
+                write_part(h, at, *fold(h, at, 0, 4096))
 
         @pl.when(i < 3)
         def _():
             y_part(h, i + 1).start()
 
-        @pl.when(jnp.logical_and(h < 2, i == 1))
-        def _():
-            share(h + 1, 1)
-            share(h + 1, 3)
-
-        @pl.when(jnp.logical_and(h < 2, i == 2))
-        def _():
-            share(h + 1, 2)
-
-        @pl.when(jnp.logical_and(h < 2, i == 3))
-        def _():
-            for d in (0, 1, 3, 2):
-                c_keys_in(h + 1, d).wait_recv()
+        @pl.when(t == 0)
+        def _():
+            share(2, 1, 3)
+
+        @pl.when(t == 1)
+        def _():
+            share(2, 2)
+
+        for own in (1, 2):
+            @pl.when(t == own * 4 - 1)
+            def _():
+                shared(own, 0, 1, 3, 2)
 
         @pl.when(jnp.logical_and(h > 0, i == 1))
         def _():
@@ -360,11 +410,21 @@
     out_copy.wait()
     head_copy.wait()
     tail_copy.wait()
-    for h in range(3):
+    for h in range(2):
         for d in (1, 3, 2):
             x_back_in(h, d).wait_recv()
-    attended = jnp.concatenate([out[n] for n in range(12)], axis=1)
-    attn_out = jnp.dot(attended, ow_buf[...], preferred_element_type=jnp.float32)
+    attn_out = jnp.zeros((128, 1536), jnp.float32)
+    for g in range(4):
+        pair = jnp.concatenate([out[g * 3], out[g * 3 + 1]], axis=1)
+        attn_out = attn_out + jnp.dot(pair, ow_buf[g * 384:g * 384 + 256, :],
+                                      preferred_element_type=jnp.float32)
+    proj_buf[...] = attn_out
+    for d in (1, 3, 2):
+        x_back_in(2, d).wait_recv()
+    last = jnp.concatenate([out[g * 3 + 2] for g in range(4)], axis=1)
+    last_weight = jnp.concatenate(
+        [ow_buf[g * 384 + 256:g * 384 + 384, :] for g in range(4)], axis=0)
+    attn_out = proj_buf[...] + jnp.dot(last, last_weight, preferred_element_type=jnp.float32)
     residual = hidden_buf[...] + table_buf[2, pl.ds(level_now, 1), :] * attn_out
     velocity = dot_nt(hw_buf[...], residual.astype(jnp.bfloat16))
     vel_out[...] = velocity
@@ -456,6 +516,8 @@
             pltpu.VMEM((128, 1536), f32),
             pltpu.VMEM((128, 1536), bf16),
             pltpu.VMEM((128, 1536), f32),
+            pltpu.VMEM((4, 512, 128), f32),
+            pltpu.VMEM((4, 512, 128), f32),
             pltpu.VMEM((4, 4, 8, 128), f32),
             pltpu.VMEM((64, 128), f32),
             pltpu.VMEM((64, 128), f32),

time: 198 us -> 195 us (0.985)
  Pallas kernels: 194 us -> 191 us
    pallas_call x2, Pallas kernels: 194 us -> 191 us  [block(): pl.pallas_call(functools.partial(block_kernel, careful), out_shape=[jax.S...]
where the time goes in v4:
time: 195 us
  Pallas kernels  191 us (98%)
    pallas_call x2, Pallas kernels, block(): pl.pallas_call(functools.partial(block_kernel, careful), out_shape=[jax.S...  191 us

profile of v4, /device:TPU:1, one launch (start us, length us, event | category | flops | bytes accessed | tf_op | source)
XLA Modules:
  0.0 194.8 jit_solution(17601924321459254843)
XLA Ops:
  0.6 0.0 copy-start
  0.6 0.0 copy-start.1
  0.7 0.0 copy-start.2
  0.7 0.0 copy-start.3
  0.7 0.0 copy-start.4
  0.7 0.0 copy-start.5
  0.7 0.0 copy-start.6
  0.7 81.0 %shard_map.121 = (f32[64,128]{1,0:T(8,128)S(1)}, f32[64,128]{1,0:T(8,128)S(1)}, f32[4,128]{1,0:T(4,128)S(1)}, s32[1]{0:T(128)}) custom-call(f32[64,128]{1,0:T(8,128)} %bitcast.19, s32[16]{0:T(128)} %step_in.1, f32[64,128]{1,0:T(8,128)} %bitcast.21, bf16[64,1536]{1,0:T(8,128)(2,1)} %patch_in.1, f32[3,64,1536]{2,1,0:T(8,128)} %bitcast.15, ...), custom_call_target="tpu_custom_call" | custom-call | flops 16000000000 | bytes 40000000 | tf_op jit(solution)/shard_map/pallas_call | solution.py:492
  82.3 0.0 copy-done
  82.3 0.0 copy-done.1
  82.3 0.0 copy-done.2
  82.3 0.0 copy-done.3
  82.3 0.0 copy-done.4
  82.3 0.0 copy-done.5
  82.4 0.0 copy-done.6
  82.4 110.6 %conditional.1 = ((f32[64,128]{1,0:T(8,128)S(1)}, f32[64,128]{1,0:T(8,128)S(1)}, f32[4,128]{1,0:T(4,128)S(1)})) conditional(s32[]{:T(128)} %bitcast.5, (f32[64,128]{1,0:T(8,128)S(1)}, s32[16]{0:T(128)S(1)}, f32[64,128]{1,0:T(8,128)}, bf16[64,1536]{1,0:T(8,128)(2,1)S(1)}, f32[3,64,1536]{2,1,0:T(8,128)S(1)}, /*index=5*/bf16[1536,4608]{1,0:T(8,128)(2,1)}, ...), branch_computations={%region_0.0_spmd, %region_1.0_spmd} | conditional | flops 16000000000 | bytes 40000032 | solution.py:552
  82.6 110.2 %branch_0_fun.1 = (f32[64,128]{1,0:T(8,128)S(1)}, f32[64,128]{1,0:T(8,128)S(1)}, f32[4,128]{1,0:T(4,128)S(1)}, s32[1]{0:T(128)}) custom-call(f32[64,128]{1,0:T(8,128)S(1)} %get-tuple-element.26.latent_in, s32[16]{0:T(128)S(1)} %get-tuple-element.27.step_in, f32[64,128]{1,0:T(8,128)} %get-tuple-element.28.tail_hbm, ...), custom_call_target="tpu_custom_call" | custom-call | flops 16000000000 | bytes 40000000 | tf_op jit(solution)/shard_map/cond/branch_0_fun/pallas_call | solution.py:492
  193.0 0.6 copy.22
  193.6 0.6 copy.23
  194.2 0.6 copy.24
Async XLA Ops:
  0.6 81.7 %copy-start = (bf16[1536,1536]{1,0:T(8,128)(2,1)S(1)}, bf16[1536,1536]{1,0:T(8,128)(2,1)}, u32[]{:S(2)}) copy-start(bf16[1536,1536]{1,0:T(8,128)(2,1)} %out_hbm.1) | copy-start | bytes 14155780
  0.6 81.7 %copy-start.1 = (f32[64,3,1536]{2,0,1:T(8,128)S(1)}, f32[64,3,1536]{2,0,1:T(8,128)}, u32[]{:S(2)}) copy-start(f32[64,3,1536]{2,0,1:T(8,128)} %param.16) | copy-start | bytes 3538948
  0.7 81.7 %copy-start.2 = (bf16[64,1536]{1,0:T(8,128)(2,1)S(1)}, bf16[64,1536]{1,0:T(8,128)(2,1)}, u32[]{:S(2)}) copy-start(bf16[64,1536]{1,0:T(8,128)(2,1)} %patch_in.1) | copy-start | bytes 589828
  0.7 81.7 %copy-start.3 = (f32[1,128,64]{1,2,0:T(8,128)S(1)}, f32[1,128,64]{1,2,0:T(8,128)}, u32[]{:S(2)}) copy-start(f32[1,128,64]{1,2,0:T(8,128)} %param.12) | copy-start | bytes 98308
  0.7 81.7 %copy-start.4 = (f32[1536]{0:T(1024)S(1)}, f32[1536]{0:T(1024)}, u32[]{:S(2)}) copy-start(f32[1536]{0:T(1024)} %q_gain_in.1) | copy-start | bytes 18436
  0.7 81.7 %copy-start.5 = (f32[1536]{0:T(1024)S(1)}, f32[1536]{0:T(1024)}, u32[]{:S(2)}) copy-start(f32[1536]{0:T(1024)} %k_gain_in.1) | copy-start | bytes 18436
  0.7 81.7 %copy-start.6 = (s32[16]{0:T(128)S(1)}, s32[16]{0:T(128)}, u32[]{:S(2)}) copy-start(s32[16]{0:T(128)} %step_in.1) | copy-start | bytes 196

commit v5 on v4

--- a/solution.py
+++ b/solution.py
@@ -79,31 +79,32 @@
         return remote(q_in.at[mine * 3 + h], q_all.at[h, 0, rows(hop(mine, -d), 128)],
                       xq_s.at[h, d], xq_r.at[h, d], peer(h, -d))
 
-    def x_keys(h, d):
-        mine = coordinate(h)
-        return remote(kv_in.at[hop(mine, d) * 3 + h], kv_all.at[h, :, rows(core * 4 + mine, 128)],
-                      xk_s.at[h, d], xk_r.at[h, d], peer(h, d))
-
-    def x_keys_in(h, d):
-        mine = coordinate(h)
-        return remote(kv_in.at[mine * 3 + h],
-                      kv_all.at[h, :, rows(core * 4 + hop(mine, -d), 128)],
-                      xk_s.at[h, d], xk_r.at[h, d], peer(h, -d))
+    def x_keys(h, d, kv):
+        mine = coordinate(h)
+        return remote(kv_in.at[kv, hop(mine, d) * 3 + h],
+                      kv_all.at[h, kv, rows(core * 4 + mine, 128)],
+                      xk_s.at[kv, h, d], xk_r.at[kv, h, d], peer(h, d))
+
+    def x_keys_in(h, d, kv):
+        mine = coordinate(h)
+        return remote(kv_in.at[kv, mine * 3 + h],
+                      kv_all.at[h, kv, rows(core * 4 + hop(mine, -d), 128)],
+                      xk_s.at[kv, h, d], xk_r.at[kv, h, d], peer(h, -d))
 
     def y_query(h, d, arriving=False):
         return remote(q_all.at[h, 0], q_all.at[h, 4 - d], yq_s.at[h, d], yq_r.at[h, d],
                       peer(turned(h, 1), -d if arriving else d))
 
-    def key_place(h, d, half):
-        return kv_all.at[h, :, rows(place[(4 - d) % 4] * 2 + half, 512)]
-
-    def z_keys(h, d, arriving=False):
-        return remote(key_place(h, 0, core), key_place(h, d, core), zk_s.at[h, d],
-                      zk_r.at[h, d], peer(turned(h, 2), -d if arriving else d))
-
-    def c_keys(h, d, arriving=False):
-        at = key_place(h, d, 1 - core if arriving else core)
-        return remote(at, at, ck_s.at[h, d], ck_r.at[h, d], device(x, y, z, 1 - core))
+    def key_place(h, d, kv, half):
+        return kv_all.at[h, kv, rows(place[(4 - d) % 4] * 2 + half, 512)]
+
+    def z_keys(h, d, kv, arriving=False):
+        return remote(key_place(h, 0, kv, core), key_place(h, d, kv, core), zk_s.at[kv, h, d],
+                      zk_r.at[kv, h, d], peer(turned(h, 2), -d if arriving else d))
+
+    def c_keys(h, d, kv, arriving=False):
+        at = key_place(h, d, kv, 1 - core if arriving else core)
+        return remote(at, at, ck_s.at[kv, h, d], ck_r.at[kv, h, d], device(x, y, z, 1 - core))
 
     def y_part(h, d, arriving=False):
         return remote(o_send.at[h, d], o_recv.at[h, 4 - d], oy_s.at[h, d], oy_r.at[h, d],
@@ -155,7 +156,7 @@
     table_copy = pltpu.make_async_copy(table_hbm, table_buf, table_sem)
     weight(3).start()
     table_copy.start()
-    for b in (4, 5, 6, 7, 8, 0, 1, 2):
+    for b in (4, 5, 0, 1, 2, 6, 7, 8):
         weight(b).start()
     barrier = pltpu.get_barrier_semaphore()
     for n in range(1, 16):
@@ -184,66 +185,30 @@
         proj_buf[:, at * 512:(at + 1) * 512] = part
         return jnp.sum(part * part, axis=-1, keepdims=True)
 
-    def pick():
-        row = lax.broadcasted_iota(jnp.int32, (1536, 128), 0)
-        lane = lax.broadcasted_iota(jnp.int32, (1536, 128), 1)
-        return jnp.logical_and(row >= lane * 128, row < lane * 128 + 128).astype(jnp.bfloat16)
-
-    def top_norm(values):
-        wide = values.astype(jnp.float32)
-        sums = jnp.dot((wide * wide).astype(jnp.bfloat16), pick(),
-                       preferred_element_type=jnp.float32)
-        return jnp.max(sums, axis=0, keepdims=True) * 1.01
-
-    square = project(3, 0) + project(4, 1) + project(5, 2)
-    factor = lax.rsqrt(square * (1.0 / 1536) + 1e-06)
-    keys = (proj_buf[...] * factor * k_gain_in[...].reshape(1, 1536)).astype(jnp.bfloat16)
-    for n in range(12):
-        kv_in[n, 0] = keys[:, n * 128:(n + 1) * 128]
-    key_size = top_norm(keys)
-    top = jnp.zeros((128, 128), jnp.float32)
-    for b in range(3):
-        weight(6 + b).wait()
-        part = jnp.dot(normed_buf[...], w_buf[6 + b], preferred_element_type=jnp.float32)
-        part = part * VALUE_SHRINK
-        for n in range(4):
-            piece = part[:, n * 128:(n + 1) * 128]
-            top = jnp.maximum(top, jnp.abs(piece))
-            kv_in[b * 4 + n, 1] = piece.astype(jnp.bfloat16)
-    value_size = jnp.max(top, axis=0, keepdims=True)
-
-    pl.semaphore_wait(barrier, 20)
-    for h in range(3):
+    def top_norm(heads):
+        lane = lax.broadcasted_iota(jnp.int32, (1, 128), 1)
+        row = jnp.zeros((1, 128), jnp.float32)
+        for n in range(12):
+            wide = heads[n].astype(jnp.float32)
+            most = jnp.max(jnp.sum(wide * wide, axis=-1, keepdims=True), axis=0, keepdims=True)
+            row = jnp.where(lane == n, most, row)
+        return row * 1.01
+
+    def scatter_keys(kv):
         for d in (1, 3, 2):
-            x_keys(h, d).start()
-    for h in range(3):
-        mine = coordinate(h)
-        for kv in range(2):
-            kv_all[h, kv, rows(core * 4 + mine, 128), :] = kv_in[mine * 3 + h, kv]
-
-    square = project(0, 0) + project(1, 1) + project(2, 2)
-    out_copy.start()
-    head_copy.start()
-    tail_copy.start()
-    factor = lax.rsqrt(square * (1.0 / 1536) + 1e-06) * (HEAD_DIM ** (-0.5) * LOG2E)
-    queries = (proj_buf[...] * factor * q_gain_in[...].reshape(1, 1536)).astype(jnp.bfloat16)
-    for n in range(12):
-        q_in[n] = queries[:, n * 128:(n + 1) * 128]
-    for h in range(3):
+            for h in range(3):
+                x_keys(h, d, kv).start()
+        for h in range(3):
+            mine = coordinate(h)
+            kv_all[h, kv, rows(core * 4 + mine, 128), :] = kv_in[kv, mine * 3 + h]
+
+    def spread_keys(h, kv):
         for d in (1, 3, 2):
-            x_query(h, d).start()
-        q_all[h, 0, rows(coordinate(h), 128), :] = q_in[coordinate(h) * 3 + h]
-    size_buf[0, 0] = jnp.concatenate(
-        [top_norm(queries), key_size, value_size, jnp.zeros((5, 128), jnp.float32)], axis=0)
-    size_send(0)
-
-    def spread_keys(h):
-        for d in (1, 3, 2):
-            x_keys_in(h, d).wait_recv()
+            x_keys_in(h, d, kv).wait_recv()
         for d in (1, 3):
-            z_keys(h, d).start()
-        c_keys(h, 0).start()
-        z_keys(h, 2).start()
+            z_keys(h, d, kv).start()
+        c_keys(h, 0, kv).start()
+        z_keys(h, 2, kv).start()
 
     def spread_queries(h):
         for d in (1, 3, 2):
@@ -252,22 +217,58 @@
             y_query(h, d).start()
 
     def share(h, *steps):
-        for d in steps:
-            z_keys(h, d, True).wait_recv()
-            c_keys(h, d).start()
+        for kv in range(2):
+            for d in steps:
+                z_keys(h, d, kv, True).wait_recv()
+                c_keys(h, d, kv).start()
 
     def shared(h, *steps):
-        for d in steps:
-            c_keys(h, d, True).wait_recv()
-
-    spread_keys(0)
-    spread_keys(1)
-    spread_queries(0)
-    spread_keys(2)
-    spread_queries(1)
-    spread_queries(2)
-    share(0, 1, 3)
-    shared(0, 0, 1, 3)
+        for kv in range(2):
+            for d in steps:
+                c_keys(h, d, kv, True).wait_recv()
+
+    square = project(3, 0) + project(4, 1) + project(5, 2)
+    factor = lax.rsqrt(square * (1.0 / 1536) + 1e-06)
+    keys = (proj_buf[...] * factor * k_gain_in[...].reshape(1, 1536)).astype(jnp.bfloat16)
+    for n in range(12):
+        kv_in[0, n] = keys[:, n * 128:(n + 1) * 128]
+    pl.semaphore_wait(barrier, 20)
+    scatter_keys(0)
+
+    square = project(0, 0) + project(1, 1) + project(2, 2)
+    factor = lax.rsqrt(square * (1.0 / 1536) + 1e-06) * (HEAD_DIM ** (-0.5) * LOG2E)
+    queries = (proj_buf[...] * factor * q_gain_in[...].reshape(1, 1536)).astype(jnp.bfloat16)
+    for n in range(12):
+        q_in[n] = queries[:, n * 128:(n + 1) * 128]
+    for d in (1, 3, 2):
+        for h in range(3):
+            x_query(h, d).start()
+    for h in range(3):
+        q_all[h, 0, rows(coordinate(h), 128), :] = q_in[coordinate(h) * 3 + h]
+    for h in range(3):
+        spread_keys(h, 0)
+
+    for b in range(3):
+        weight(6 + b).wait()
+        part = jnp.dot(normed_buf[...], w_buf[6 + b], preferred_element_type=jnp.float32)
+        part = (part * VALUE_SHRINK).astype(jnp.bfloat16)
+        for n in range(4):
+            kv_in[1, b * 4 + n] = part[:, n * 128:(n + 1) * 128]
+    out_copy.start()
+    head_copy.start()
+    tail_copy.start()
+    scatter_keys(1)
+    for h in range(3):
+        spread_queries(h)
+
+    top = functools.reduce(jnp.maximum, [jnp.abs(kv_in[1, n].astype(jnp.float32))
+                                         for n in range(12)])
+    size_buf[0, 0] = jnp.concatenate(
+        [top_norm(q_in[...]), top_norm(kv_in[0]), jnp.max(top, axis=0, keepdims=True),
+         jnp.zeros((5, 128), jnp.float32)], axis=0)
+    for h in range(3):
+        spread_keys(h, 1)
+    size_send(0)
 
     def combine(h):
         for d in (1, 2, 3):
@@ -325,60 +326,65 @@
         tail = jnp.concatenate(two(as_rows(den, jnp.sum)) + two(top), axis=0)
         o_send[h, at, 512:528, :] = tail.astype(jnp.bfloat16)
 
-    def early(at, carry):
-        for d in (1, 2, 3):
-            @pl.when(at == 4 - d)
-            def _():
-                y_query(0, d, True).wait_recv()
+    def early(e, carry):
+        r, h = e // 3, lax.rem(e, 3)
+        at = r + r // 2
+
+        @pl.when(r == 0)
+        def _():
+            shared(h, 0)
+
+        @pl.when(r > 0)
+        def _():
+            y_query(h, 4 - at, True).wait_recv()
 
         if not careful:
-            num, den, _ = fold(0, at, 0, 3072)
-            num_buf[at] = num
-            den_buf[at] = den
-
-        @pl.when(at == 1)
-        def _():
-            share(0, 2)
+            num, den, _ = fold(h, at, 0, 1024)
+            num_buf[h, at] = num
+            den_buf[h, at] = den
+
+        @pl.when(e == 6)
+        def _():
+            share(0, 1, 3)
+
+        @pl.when(e == 7)
+        def _():
+            share(1, 1, 3)
+
+        return carry
+
+    lax.fori_loop(0, 9, early, 0)
+    share(0, 2)
+    shared(0, 1, 3, 2)
+
+    def chunk(t, carry):
+        h = jnp.where(t < 4, 0, jnp.where(t < 10, (t - 1) // 3, t - 9))
+        i = jnp.where(t < 4, t, jnp.where(t < 10, lax.rem(t - 1, 3), 3))
+        at = lax.rem(i + 1, 4)
 
         @pl.when(at == 2)
         def _():
-            share(1, 1, 3)
-
-        @pl.when(at == 3)
-        def _():
-            share(1, 2)
-
-        return carry
-
-    lax.fori_loop(0, 4, early, 0)
-    shared(0, 2)
-
-    def chunk(t, carry):
-        h, i = t // 4, lax.rem(t, 4)
-        at = lax.rem(i + 1, 4)
-
-        @pl.when(jnp.logical_and(h > 0, i < 3))
-        def _():
-            y_query(h, 3 - i, True).wait_recv()
+            y_query(h, 2, True).wait_recv()
 
         if careful:
             write_part(h, at, *fold(h, at, 0, 4096))
         else:
-            @pl.when(h == 0)
-            def _():
-                num, den, top = fold(0, at, 3072, 4096)
-                write_part(0, at, num_buf[at] + num, den_buf[at] + den, top)
-
-            @pl.when(h > 0)
+            @pl.when(at == 2)
             def _():
                 write_part(h, at, *fold(h, at, 0, 4096))
 
+            @pl.when(at != 2)
+            def _():
+                num, den, top = fold(h, at, 1024, 4096)
+                write_part(h, at, num_buf[h, at] + num, den_buf[h, at] + den, top)
+
         @pl.when(i < 3)
         def _():
             y_part(h, i + 1).start()
 
         @pl.when(t == 0)
         def _():
+            share(1, 2)
             share(2, 1, 3)
 
         @pl.when(t == 1)
@@ -386,13 +392,13 @@
             share(2, 2)
 
         for own in (1, 2):
-            @pl.when(t == own * 4 - 1)
+            @pl.when(t == own * 3)
             def _():
-                shared(own, 0, 1, 3, 2)
-
-        @pl.when(jnp.logical_and(h > 0, i == 1))
-        def _():
-            combine(h - 1)
+                shared(own, 1, 3, 2)
+
+            @pl.when(t == own * 5)
+            def _():
+                combine(own - 1)
 
         for stage in range(3):
             @pl.when(t == 2 * stage + 2)
@@ -474,18 +480,21 @@
             size_step(stage, d).wait_send()
     for h in range(3):
         for d in (1, 2, 3):
-            x_keys(h, d).wait_send()
+            for kv in range(2):
+                x_keys(h, d, kv).wait_send()
+                z_keys(h, d, kv).wait_send()
             x_query(h, d).wait_send()
             y_query(h, d).wait_send()
-            z_keys(h, d).wait_send()
             y_part(h, d).wait_send()
             x_back(h, d).wait_send()
         for d in range(4):
-            c_keys(h, d).wait_send()
+            for kv in range(2):
+                c_keys(h, d, kv).wait_send()
 
 
 def block(careful, *operands):
-    sems = [pltpu.SemaphoreType.DMA((3, 4))] * 14
+    one, both = pltpu.SemaphoreType.DMA((3, 4)), pltpu.SemaphoreType.DMA((2, 3, 4))
+    sems = [one] * 2 + [both] * 2 + [one] * 2 + [both] * 4 + [one] * 4
     vmem, hbm = pl.BlockSpec(memory_space=pltpu.VMEM), pl.BlockSpec(memory_space=pltpu.HBM)
     smem = pl.BlockSpec(memory_space=pltpu.SMEM)
     f32, bf16, dma = jnp.float32, jnp.bfloat16, pltpu.SemaphoreType.DMA
@@ -501,7 +510,7 @@
         out_specs=[vmem, vmem, vmem, smem],
         scratch_shapes=[
             pltpu.VMEM((12, 128, 128), bf16),
-            pltpu.VMEM((12, 2, 128, 128), bf16),
+            pltpu.VMEM((2, 12, 128, 128), bf16),
             pltpu.VMEM((3, 4, 512, 128), bf16),
             pltpu.VMEM((3, 2, 4096, 128), bf16),
             pltpu.VMEM((3, 4, 528, 128), bf16),
@@ -516,8 +525,8 @@
             pltpu.VMEM((128, 1536), f32),
             pltpu.VMEM((128, 1536), bf16),
             pltpu.VMEM((128, 1536), f32),
-            pltpu.VMEM((4, 512, 128), f32),
-            pltpu.VMEM((4, 512, 128), f32),
+            pltpu.VMEM((3, 4, 512, 128), f32),
+            pltpu.VMEM((3, 4, 512, 128), f32),
             pltpu.VMEM((4, 4, 8, 128), f32),
             pltpu.VMEM((64, 128), f32),
             pltpu.VMEM((64, 128), f32),

time: 195 us -> 194 us (level)
  no operation moved by 1% of the time
where the time goes in v5:
time: 194 us
  Pallas kernels  191 us (98%)
    pallas_call x2, Pallas kernels, block(): pl.pallas_call(functools.partial(block_kernel, careful), out_shape=[jax.S...  191 us

profile of v5, /device:TPU:1, one launch (start us, length us, event | category | flops | bytes accessed | tf_op | source)
XLA Modules:
  0.0 194.3 jit_solution(7076680845463436122)
XLA Ops:
  0.6 0.0 copy-start
  0.6 0.0 copy-start.1
  0.7 0.0 copy-start.2
  0.7 0.0 copy-start.3
  0.7 0.0 copy-start.4
  0.7 0.0 copy-start.5
  0.7 0.0 copy-start.6
  0.7 76.8 %shard_map.121 = (f32[64,128]{1,0:T(8,128)S(1)}, f32[64,128]{1,0:T(8,128)S(1)}, f32[4,128]{1,0:T(4,128)S(1)}, s32[1]{0:T(128)}) custom-call(f32[64,128]{1,0:T(8,128)} %bitcast.19, s32[16]{0:T(128)} %step_in.1, f32[64,128]{1,0:T(8,128)} %bitcast.21, bf16[64,1536]{1,0:T(8,128)(2,1)} %patch_in.1, f32[3,64,1536]{2,1,0:T(8,128)} %bitcast.15, ...), custom_call_target="tpu_custom_call" | custom-call | flops 16000000000 | bytes 40000000 | tf_op jit(solution)/shard_map/pallas_call | solution.py:501
  78.1 0.0 copy-done
  78.1 0.0 copy-done.1
  78.2 0.0 copy-done.2
  78.2 0.0 copy-done.3
  78.2 0.0 copy-done.4
  78.2 0.0 copy-done.5
  78.2 0.0 copy-done.6
  78.2 114.3 %conditional.1 = ((f32[64,128]{1,0:T(8,128)S(1)}, f32[64,128]{1,0:T(8,128)S(1)}, f32[4,128]{1,0:T(4,128)S(1)})) conditional(s32[]{:T(128)} %bitcast.5, (f32[64,128]{1,0:T(8,128)S(1)}, s32[16]{0:T(128)S(1)}, f32[64,128]{1,0:T(8,128)}, bf16[64,1536]{1,0:T(8,128)(2,1)S(1)}, f32[3,64,1536]{2,1,0:T(8,128)S(1)}, /*index=5*/bf16[1536,4608]{1,0:T(8,128)(2,1)}, ...), branch_computations={%region_0.0_spmd, %region_1.0_spmd} | conditional | flops 16000000000 | bytes 40000032 | solution.py:561
  78.4 113.9 %branch_0_fun.1 = (f32[64,128]{1,0:T(8,128)S(1)}, f32[64,128]{1,0:T(8,128)S(1)}, f32[4,128]{1,0:T(4,128)S(1)}, s32[1]{0:T(128)}) custom-call(f32[64,128]{1,0:T(8,128)S(1)} %get-tuple-element.26.latent_in, s32[16]{0:T(128)S(1)} %get-tuple-element.27.step_in, f32[64,128]{1,0:T(8,128)} %get-tuple-element.28.tail_hbm, ...), custom_call_target="tpu_custom_call" | custom-call | flops 16000000000 | bytes 40000000 | tf_op jit(solution)/shard_map/cond/branch_0_fun/pallas_call | solution.py:501
  192.5 0.6 copy.22
  193.1 0.6 copy.23
  193.7 0.6 copy.24
Async XLA Ops:
  0.6 77.5 %copy-start = (bf16[1536,1536]{1,0:T(8,128)(2,1)S(1)}, bf16[1536,1536]{1,0:T(8,128)(2,1)}, u32[]{:S(2)}) copy-start(bf16[1536,1536]{1,0:T(8,128)(2,1)} %out_hbm.1) | copy-start | bytes 14155780
  0.6 77.5 %copy-start.1 = (f32[64,3,1536]{2,0,1:T(8,128)S(1)}, f32[64,3,1536]{2,0,1:T(8,128)}, u32[]{:S(2)}) copy-start(f32[64,3,1536]{2,0,1:T(8,128)} %param.16) | copy-start | bytes 3538948
  0.7 77.5 %copy-start.2 = (bf16[64,1536]{1,0:T(8,128)(2,1)S(1)}, bf16[64,1536]{1,0:T(8,128)(2,1)}, u32[]{:S(2)}) copy-start(bf16[64,1536]{1,0:T(8,128)(2,1)} %patch_in.1) | copy-start | bytes 589828
  0.7 77.5 %copy-start.3 = (f32[1,128,64]{1,2,0:T(8,128)S(1)}, f32[1,128,64]{1,2,0:T(8,128)}, u32[]{:S(2)}) copy-start(f32[1,128,64]{1,2,0:T(8,128)} %param.12) | copy-start | bytes 98308
  0.7 77.5 %copy-start.4 = (f32[1536]{0:T(1024)S(1)}, f32[1536]{0:T(1024)}, u32[]{:S(2)}) copy-start(f32[1536]{0:T(1024)} %q_gain_in.1) | copy-start | bytes 18436
  0.7 77.5 %copy-start.5 = (f32[1536]{0:T(1024)S(1)}, f32[1536]{0:T(1024)}, u32[]{:S(2)}) copy-start(f32[1536]{0:T(1024)} %k_gain_in.1) | copy-start | bytes 18436
  0.7 77.5 %copy-start.6 = (s32[16]{0:T(128)S(1)}, s32[16]{0:T(128)}, u32[]{:S(2)}) copy-start(s32[16]{0:T(128)} %step_in.1) | copy-start | bytes 196
